TPU v7x, 128 devices: a whole 4x4x4 slice. The times are simulated.
128 devices in a mesh: dp: 8 (over y_hi, z), fsdp: 16 (over y_lo, x, core).
Axes of the slice: x: 4, y: 4 (y_hi: 2, y_lo: 2; y = y_hi * 2 + y_lo), z: 4, core: 2. Of those that a mesh axis runs over, the one named last changes fastest.
Arguments:
- tokens: bfloat16 [65536, 1024], P(('dp', 'fsdp')), may hold values from -24 to 24
- lengths: int32 [128], replicated, may hold values from 1 to 512, 40960 in all
- placement_ids: int32 [128], P(('dp', 'fsdp')), may hold values from 0 to 127, each once
- norm_gain: bfloat16 [1024], P(('dp', 'fsdp')), may hold values from 0.5 to 1.5
- in_weight: bfloat16 [1024, 4384], P(('dp', 'fsdp')), may hold values from -0.1875 to 0.1875
- conv_weight: bfloat16 [4, 2304], P(None, ('dp', 'fsdp')), may hold values from -3 to 3
- conv_bias: bfloat16 [2304], P(('dp', 'fsdp')), may hold values from -4 to 4
- dt_bias: float32 [32], replicated, may hold values from -4 to -1
- a_log: float32 [32], replicated, may hold values from -3 to 1
- d_skip: float32 [32], replicated, may hold values from 0.5 to 1.5
- inner_gain: bfloat16 [2048], P(('dp', 'fsdp')), may hold values from 0.5 to 1.5
- out_weight: bfloat16 [2048, 1024], P(('dp', 'fsdp')), may hold values from -0.125 to 0.125
- cotangent: bfloat16 [65536, 1024], P(('dp', 'fsdp')), may hold values from -6 to 6
Outputs:
- block_out: bfloat16 [65536, 1024], P(('dp', 'fsdp'))
- input_grad: bfloat16 [65536, 1024], P(('dp', 'fsdp'))
- norm_gain_grad: float32 [1024], P(('dp', 'fsdp'))
- in_weight_grad: float32 [1024, 4384], P(('dp', 'fsdp'))
- conv_weight_grad: float32 [4, 2304], P(None, ('dp', 'fsdp'))
- conv_bias_grad: float32 [2304], P(('dp', 'fsdp'))
- dt_bias_grad: float32 [32], replicated
- a_log_grad: float32 [32], replicated
- d_skip_grad: float32 [32], replicated
- inner_gain_grad: float32 [2048], P(('dp', 'fsdp'))
- out_weight_grad: float32 [2048, 1024], P(('dp', 'fsdp'))
Inputs may be any that keep to these rules, and one draw needn't show every extreme that they name: Sequence j has lengths[j] live slots at the start of its slot and padding after them. Some sequence is exactly 512 long. `placement_ids`: each sequence is held by exactly one slot.
All inputs are finite; a program needn't handle non-finite values.
Results may differ from a plain program's by a relative error of at most 0.0072.
Values may be sent and summed in bfloat16 or wider, within the bound.
A program may use at most 192 MiB of HBM per device.

v0:
```python
import jax
import jax.numpy as jnp
from jax import lax
from jax.sharding import PartitionSpec as P

D = 1024
INNER = 2048
STATE = 128
HEAD = 64
CONV = 4
MB = 2
HEADS = 32
XBC = 2304
PROJ = 4384


eps = 1e-05
highest = lax.Precision.HIGHEST


def scaled_rows(values, gains):
    return values * lax.rsqrt(jnp.mean(values * values, axis=-1, keepdims=True) + eps) * gains


def rounded(values):
    return lax.optimization_barrier(values.astype(jnp.bfloat16)).astype(jnp.float32)


def convolve(inputs, tail_rows, conv_taps, conv_shift):
    count_rows = inputs.shape[0]
    padded = jnp.concatenate([tail_rows, inputs], axis=0)
    summed = conv_shift + conv_taps[0] * padded[0:count_rows]
    for offset in range(1, CONV):
        summed = summed + conv_taps[offset] * padded[offset : offset + count_rows]
    return jax.nn.silu(summed)


def state_mix(values, key_cols, query_cols, step_sizes, decay_rates, skip_gains, state_in):
    count_rows = values.shape[0]
    cumulative = jnp.cumsum(step_sizes * decay_rates, axis=0)
    intersections = jnp.dot(query_cols, key_cols.T, precision=highest)
    causal = lax.broadcasted_iota(jnp.int32, (count_rows, count_rows), 0) >= lax.broadcasted_iota(
        jnp.int32, (count_rows, count_rows), 1
    )
    log_gaps = cumulative.T[:, :, None] - cumulative.T[:, None, :]
    decays = jnp.exp(jnp.where(causal[None], log_gaps, -1e30))
    mixing = intersections[None] * decays * step_sizes.T[:, None, :]
    outputs = jnp.einsum("hts,shp->thp", mixing, values, precision=highest)
    carried = (
        jnp.einsum("tn,hpn->thp", query_cols, state_in, precision=highest)
        * jnp.exp(cumulative)[:, :, None]
    )
    last_weights = jnp.exp(cumulative[-1][None, :] - cumulative) * step_sizes
    state_out = jnp.exp(cumulative[-1])[:, None, None] * state_in + jnp.einsum(
        "sh,shp,sn->hpn", last_weights, values, key_cols, precision=highest
    )
    return (outputs + carried + skip_gains[None, :, None] * values, state_out)


def mixer_piece(
    activated, gate_cols, step_raw, shift_heads, rate_logs, skip_gains, inner_gains, state_in
):
    count_rows = activated.shape[0]
    values = activated[:, :INNER].reshape(count_rows, HEADS, HEAD)
    key_cols = activated[:, INNER : INNER + STATE]
    query_cols = activated[:, INNER + STATE :]
    step_sizes = jax.nn.softplus(step_raw + shift_heads)
    decay_rates = -jnp.exp(rate_logs)
    mixed, state_out = state_mix(
        values, key_cols, query_cols, step_sizes, decay_rates, skip_gains, state_in
    )
    gated_rows = mixed.reshape(count_rows, INNER) * jax.nn.silu(gate_cols)
    return (scaled_rows(gated_rows, inner_gains), state_out)


def body(
    tokens,
    lengths,
    placement_ids,
    norm_gain,
    in_weight,
    conv_weight,
    conv_bias,
    dt_bias,
    a_log,
    d_skip,
    inner_gain,
    out_weight,
    cotangent,
):
    seq_rows = tokens.shape[0]
    batch_rows = seq_rows // MB
    sequence_id = placement_ids[0]
    slot_length = jnp.sum(
        jnp.where(lax.broadcasted_iota(jnp.int32, lengths.shape, 0) == sequence_id, lengths, 0)
    )
    shards = (norm_gain, in_weight, conv_weight, conv_bias, inner_gain, out_weight)
    weight_sums = (
        jnp.zeros((D,), jnp.float32),
        jnp.zeros((D, PROJ), jnp.float32),
        jnp.zeros((CONV, XBC), jnp.float32),
        jnp.zeros((XBC,), jnp.float32),
        jnp.zeros((INNER,), jnp.float32),
        jnp.zeros((INNER, D), jnp.float32),
    )
    head_sums = (jnp.zeros_like(dt_bias), jnp.zeros_like(a_log), jnp.zeros_like(d_skip))
    state_now = jnp.zeros((HEADS, HEAD, STATE), jnp.float32)
    tail_now = jnp.zeros((CONV - 1, XBC), jnp.float32)
    block_rows = []
    saved = []
    for micro_batch in range(MB):
        first_row = micro_batch * batch_rows
        inputs = tokens[first_row : first_row + batch_rows].astype(jnp.float32)
        back_rows = cotangent[first_row : first_row + batch_rows].astype(jnp.float32)
        positions = lax.broadcasted_iota(jnp.int32, (batch_rows, 1), 0) + first_row
        live_rows = (positions < slot_length).astype(jnp.float32)
        fetched = (
            lax.all_gather(shards[0], ("dp", "fsdp"), axis=0, tiled=True),
            lax.all_gather(shards[1], ("dp", "fsdp"), axis=0, tiled=True),
            lax.all_gather(shards[2], ("dp", "fsdp"), axis=1, tiled=True),
            lax.all_gather(shards[3], ("dp", "fsdp"), axis=0, tiled=True),
            lax.all_gather(shards[4], ("dp", "fsdp"), axis=0, tiled=True),
            lax.all_gather(shards[5], ("dp", "fsdp"), axis=0, tiled=True),
        )
        full_gain, full_in, full_conv, full_bias, full_inner, full_out = fetched
        normed, pull_norm = jax.vjp(scaled_rows, inputs, full_gain.astype(jnp.float32))
        normed_low = normed.astype(jnp.bfloat16)
        projected = jnp.dot(normed_low, full_in, preferred_element_type=jnp.float32)
        conv_in = projected[:, INNER : INNER + XBC]
        activated, pull_conv = jax.vjp(
            convolve,
            conv_in,
            tail_now,
            full_conv.astype(jnp.float32),
            full_bias.astype(jnp.float32),
        )
        tail_now = conv_in[batch_rows - (CONV - 1) :]
        activated_low = rounded(activated)
        mixer_result, pull_mixer = jax.vjp(
            mixer_piece,
            activated_low,
            projected[:, :INNER],
            projected[:, INNER + XBC :],
            dt_bias,
            a_log,
            d_skip,
            full_inner.astype(jnp.float32),
            state_now,
        )
        normed_inner, state_now = mixer_result
        inner_low = normed_inner.astype(jnp.bfloat16)
        branch = jnp.dot(inner_low, full_out, preferred_element_type=jnp.float32)
        block_rows.append((inputs + live_rows * branch).astype(jnp.bfloat16))
        saved.append(
            (back_rows, live_rows, normed_low, inner_low, pull_norm, pull_conv, pull_mixer)
        )
    grad_state = jnp.zeros((HEADS, HEAD, STATE), jnp.float32)
    pending_tail = jnp.zeros((CONV - 1, XBC), jnp.float32)
    grad_rows = [None] * MB
    for micro_batch in reversed(range(MB)):
        back_rows, live_rows, normed_low, inner_low, pull_norm, pull_conv, pull_mixer = saved[
            micro_batch
        ]
        back_in, back_out = (
            lax.all_gather(in_weight, ("dp", "fsdp"), axis=0, tiled=True),
            lax.all_gather(out_weight, ("dp", "fsdp"), axis=0, tiled=True),
        )
        grad_branch = (live_rows * back_rows).astype(jnp.bfloat16)
        grad_out = jnp.einsum(
            "tk,td->kd", inner_low, grad_branch, preferred_element_type=jnp.float32
        )
        grad_inner = jnp.einsum(
            "td,kd->tk", grad_branch, back_out, preferred_element_type=jnp.float32
        )
        (
            grad_act,
            grad_gate,
            grad_step,
            grad_shift,
            grad_rate,
            grad_skip,
            grad_inner_gain,
            grad_state,
        ) = pull_mixer((grad_inner, grad_state))
        grad_conv_in, grad_tail, grad_taps, grad_conv_shift = pull_conv(grad_act)
        grad_conv_in = jnp.concatenate(
            [
                grad_conv_in[: batch_rows - (CONV - 1)],
                grad_conv_in[batch_rows - (CONV - 1) :] + pending_tail,
            ],
            axis=0,
        )
        pending_tail = grad_tail
        grad_proj = jnp.concatenate([grad_gate, grad_conv_in, grad_step], axis=1).astype(
            jnp.bfloat16
        )
        grad_in = jnp.einsum("td,tk->dk", normed_low, grad_proj, preferred_element_type=jnp.float32)
        grad_normed = jnp.einsum(
            "tk,dk->td", grad_proj, back_in, preferred_element_type=jnp.float32
        )
        grad_inputs, grad_norm_gain = pull_norm(grad_normed)
        grad_rows[micro_batch] = (back_rows + grad_inputs).astype(jnp.bfloat16)
        grad_terms = (
            grad_norm_gain,
            grad_in,
            grad_taps,
            grad_conv_shift,
            grad_inner_gain,
            grad_out,
        )
        head_sums = (head_sums[0] + grad_shift, head_sums[1] + grad_rate, head_sums[2] + grad_skip)
        weight_sums = jax.tree.map(jnp.add, weight_sums, grad_terms)
    weight_sums = (
        lax.psum_scatter(weight_sums[0], ("dp", "fsdp"), scatter_dimension=0, tiled=True),
        lax.psum_scatter(weight_sums[1], ("dp", "fsdp"), scatter_dimension=0, tiled=True),
        lax.psum_scatter(weight_sums[2], ("dp", "fsdp"), scatter_dimension=1, tiled=True),
        lax.psum_scatter(weight_sums[3], ("dp", "fsdp"), scatter_dimension=0, tiled=True),
        lax.psum_scatter(weight_sums[4], ("dp", "fsdp"), scatter_dimension=0, tiled=True),
        lax.psum_scatter(weight_sums[5], ("dp", "fsdp"), scatter_dimension=0, tiled=True),
    )
    head_totals = lax.psum((head_sums[0], head_sums[1], head_sums[2]), ("dp", "fsdp"))
    block_out = jnp.concatenate(block_rows, axis=0)
    input_grad = jnp.concatenate(grad_rows, axis=0)
    return (
        block_out,
        input_grad,
        weight_sums[0],
        weight_sums[1],
        weight_sums[2],
        weight_sums[3],
        head_totals[0],
        head_totals[1],
        head_totals[2],
        weight_sums[4],
        weight_sums[5],
    )


def solution(mesh):
    placed = (
        P(("dp", "fsdp"), None),
        P(),
        P(("dp", "fsdp")),
        P(("dp", "fsdp")),
        P(("dp", "fsdp"), None),
        P(None, ("dp", "fsdp")),
        P(("dp", "fsdp")),
        P(),
        P(),
        P(),
        P(("dp", "fsdp")),
        P(("dp", "fsdp"), None),
        P(("dp", "fsdp"), None),
    )
    return jax.shard_map(
        body,
        mesh=mesh,
        in_specs=placed,
        out_specs=(
            P(("dp", "fsdp"), None),
            P(("dp", "fsdp"), None),
            P(("dp", "fsdp")),
            P(("dp", "fsdp"), None),
            P(None, ("dp", "fsdp")),
            P(("dp", "fsdp")),
            P(),
            P(),
            P(),
            P(("dp", "fsdp")),
            P(("dp", "fsdp"), None),
        ),
        check_vma=False,
    )
```

profile of v0, /device:TPU:1, one launch (start us, length us, event | category | flops | bytes accessed | tf_op | source)
XLA Modules:
  0.0 1509.9 jit_solution(15175291825334587999)
XLA Ops:
  11.9 69.0 %all-reduce.36 = (bf16[1024]{0:T(1024)(128)(2,1)S(1)}, bf16[2304]{0:T(1024)(128)(2,1)S(1)}, bf16[2048]{0:T(1024)(128)(2,1)S(1)}) all-reduce(bf16[1024]{0:T(1024)(128)(2,1)S(1)} %dynamic-update-slice.1, bf16[2304]{0:T(1024)(128)(2,1)S(1)} %dynamic-update-slice, ...), channel_id=1, replica_groups=mesh['dp'=8,'fsdp'=16] {'dp','fsdp'}, use_global_device_ids=true, to_apply=%add.28 | all-reduce | flops 5376 | bytes 21504
  81.5 173.7 %all-gather = bf16[128,18,4]{1,2,0:T(4,128)(2,1)S(1)} all-gather(bf16[1,18,4]{1,2,0:T(4,128)(2,1)} %bitcast.254), channel_id=1, replica_groups=mesh['dp'=8,'fsdp'=16] {'dp','fsdp'}, dimensions={0}, use_global_device_ids=true | all-gather | bytes 18576 | tf_op jit(solution)/shard_map/all_gather | solution.py:120
  262.3 5.2 fusion.127
  267.4 148.7 %all-gather.4.cloned.1.call-done = bf16[1024,4384]{1,0:T(8,128)(2,1)} async-done(((bf16[8,4384]{1,0:T(8,128)(2,1)}), bf16[1024,4384]{1,0:T(8,128)(2,1)}) %all-gather.4.cloned.1.call-update) | async-done | bytes 8978448 | tf_op jit(solution)/shard_map/all_gather | solution.py:119
  416.1 7.5 fusion.143
  427.1 7.5 fusion.146
  442.8 7.4 multiply_convert_fusion.1
  477.2 8.8 fusion.58
  487.3 6.3 fusion.57
  495.9 2.9 multiply_reduce_fusion.13
  498.9 5.8 multiply_reduce_fusion.15
  510.4 2.8 fusion.93
  513.2 3.0 fusion.48
  520.4 3.3 multiply_reduce_fusion.17
  523.8 5.9 fusion.202
  529.8 7.3 bitcast_add_fusion
  538.6 7.7 bitcast_add_fusion.1
  546.3 16.5 %fusion.13 = (f32[32,256]{1,0:T(8,128)}, f32[32,256]{1,0:T(8,128)}, f32[32,256]{1,0:T(8,128)}, f32[256,256]{1,0:T(8,128)S(1)}, f32[256,256]{1,0:T(8,128)S(1)}, /...) fusion(f32[32,256]{1,0:T(8,128)S(1)} %copy-done.100, f32[32,256]{1,0:T(8,128)S(1)} %copy-done.102, ...), kind=kOutput, calls=%fused_computation.18 | convolution fusion | flops 1664958464 | bytes 12976128 | tf_op jit(solution)/shard_map/transpose(jvp(hts,shp->thp))/dot_general | solution.py:48
  565.8 4.8 multiply_reduce_fusion.6
  570.7 6.6 multiply_reduce_fusion.10
  577.3 3.7 broadcast_multiply_fusion
  581.0 2.8 pad_add_fusion
  583.8 2.9 pad_add_fusion.1
  613.5 9.1 fusion.114
  622.6 16.5 %convolution_add_fusion = f32[1024,4384]{1,0:T(8,128)} fusion(f32[1024,4384]{1,0:T(8,128)} %fusion.114, bf16[256,32]{0,1:T(8,128)(2,1)S(1)} %copy.229, bf16[3,2304]{0,1:T(8,128)(2,1)S(1)} %copy-done.49, bf16[253,2304]{0,1:T(8,128)(2,1)S(1)} %slice.356, bf16[256,2048]{0,1:T(8,128)(2,1)S(1)} %copy-done.42, f32[1024]{0:T(1024)S(1)} %convert_element_type.88, ...), kind=kOutput, calls=%fused_computation | convolution fusion | flops 2312994816 | bytes 39277568 | tf_op jit(solution)/shard_map/td,tk->dk/dot_general | solution.py:197
  643.3 5.0 convolution_add_fusion.1
  649.8 8.0 fusion.141
  657.9 8.4 fusion.95
  666.4 65.3 %all-reduce.35 = (f32[1024]{0:T(1024)S(1)}, f32[4,2304]{1,0:T(4,128)S(1)}, f32[2304]{0:T(1024)S(1)}, f32[32]{0:T(128)}, f32[32]{0:T(128)}, /*index=5*/f32[32]{0:T(128)}, f32[2048]{0:T(1024)S(1)}) all-reduce(f32[1024]{0:T(1024)S(1)} %add.275, f32[4,2304]{1,0:T(4,128)S(1)} %add_add_fusion.4, ...), channel_id=2, replica_groups=mesh['dp'=8,'fsdp'=16] {'dp','fsdp'}, use_global_device_ids=true, to_apply=%region_33.35.clone | all-reduce | flops 14688 | bytes 117504
  734.1 4.4 fusion.79
  743.5 114.9 %all-reduce.39.cloned.1.call-done = f32[1024,4384]{1,0:T(8,128)} async-done(((f32[1024,4384]{1,0:T(8,128)}), f32[1024,4384]{1,0:T(8,128)}) %all-reduce.39.cloned.1.call-update) | async-done | bytes 17956880
  860.0 642.9 %reduce-scatter.3.cloned.1.call-done = f32[16,1024]{1,0:T(8,128)} async-done(((f32[2048,1024]{1,0:T(8,128)}), f32[16,1024]{1,0:T(8,128)}) %reduce-scatter.3.cloned.1.call-update) | async-done | bytes 65552 | tf_op jit(solution)/shard_map/reduce_scatter | solution.py:219
  (448 shorter events, 108.8 us)
Async XLA Ops:
  7.2 255.1 %all-gather.6.cloned.1.call-start = ((), (), s32[]{:S(2)}) async-start(), calls=%async_computation.2 | async-start | bytes 4227072 | tf_op jit(solution)/shard_map/all_gather | solution.py:123
  7.9 408.2 %all-gather.4.cloned.1.call-start = ((), (), s32[]{:S(2)}) async-start(), calls=%async_computation.1 | async-start | bytes 9246720 | tf_op jit(solution)/shard_map/all_gather | solution.py:119
  8.7 849.8 %all-reduce.39.cloned.1.call-start = ((), (), s32[]{:S(2)}) async-start(), calls=%async_computation.4 | async-start | bytes 36700160
  258.2 9.2 copy-start.127
  262.2 153.9 %copy-start.119 = (f32[256]{0:T(256)}, f32[256]{0:T(256)S(1)}, u32[]{:S(2)}) copy-start(f32[256]{0:T(256)S(1)} %get-tuple-element.140) | copy-start | bytes 3076
  262.3 153.9 %copy-start.15 = (bf16[512,1024]{1,0:T(8,128)(2,1)S(1)}, bf16[512,1024]{1,0:T(8,128)(2,1)}, u32[]{:S(2)}) copy-start(bf16[512,1024]{1,0:T(8,128)(2,1)} %param.14) | copy-start | bytes 3145732
  426.2 16.5 %copy-start.5 = (f32[256,2304]{0,1:T(8,128)}, f32[256,2304]{0,1:T(8,128)S(1)}, u32[]{:S(2)}) copy-start(f32[256,2304]{0,1:T(8,128)S(1)} %slice.181) | copy-start | bytes 7077892
  427.1 9.7 copy-start.34
  442.7 10.9 copy-start.7
  458.4 18.2 %copy-start.19 = (bf16[256,2048]{0,1:T(8,128)(2,1)}, bf16[256,2048]{0,1:T(8,128)(2,1)S(1)}, u32[]{:S(2)}) copy-start(bf16[256,2048]{0,1:T(8,128)(2,1)S(1)} %get-tuple-element.100) | copy-start | bytes 3145732
  468.3 17.7 %copy-start.17 = (f32[32,64,128]{2,1,0:T(8,128)}, f32[32,64,128]{2,1,0:T(8,128)S(1)}, u32[]{:S(2)}) copy-start(f32[32,64,128]{2,1,0:T(8,128)S(1)} %get-tuple-element.129) | copy-start | bytes 3145732
  475.6 10.4 slice-start
  477.2 8.8 slice-start.1
  477.2 9.7 copy-start.52
  486.8 12.0 copy-start.2
  486.9 12.0 copy-start.117
  529.8 8.7 copy-start.53
  538.6 27.2 %slice-start.2 = ((s8[4489216]{0:T(1024)(128)(4,1)}), s8[4194304]{0:T(1024)(128)(4,1)S(1)}, s32[]{:S(2)}) async-start(s8[4489216]{0:T(1024)(128)(4,1)} %bitcast.219), calls=%async_computation.7 | async-start | bytes 8388608
  538.6 32.0 %slice-start.6 = ((s8[4489216]{0:T(1024)(128)(4,1)}), s8[4194304]{0:T(1024)(128)(4,1)S(1)}, s32[]{:S(2)}) async-start(s8[4489216]{0:T(1024)(128)(4,1)} %bitcast.227), calls=%async_computation.11 | async-start | bytes 8388608
  546.3 16.5 %copy-start.60 = (f32[256,128]{0,1:T(8,128)S(1)}, f32[256,128]{0,1:T(8,128)}, u32[]{:S(2)}) copy-start(f32[256,128]{0,1:T(8,128)} %fusion.93) | copy-start | bytes 393220
  546.3 19.1 %copy-start.59 = (f32[256,128]{0,1:T(8,128)S(1)}, f32[256,128]{0,1:T(8,128)}, u32[]{:S(2)}) copy-start(f32[256,128]{0,1:T(8,128)} %fusion.86) | copy-start | bytes 393220
  546.3 19.5 %slice-start.3 = ((s8[4489216]{0:T(1024)(128)(4,1)}), s8[294912]{0:T(1024)(128)(4,1)S(1)}, s32[]{:S(2)}) async-start(s8[4489216]{0:T(1024)(128)(4,1)} %bitcast.219), calls=%async_computation.8 | async-start | bytes 589824
  546.3 19.5 %copy-start.23 = (f32[256,2304]{0,1:T(8,128)S(1)}, f32[256,2304]{0,1:T(8,128)}, u32[]{:S(2)}) copy-start(f32[256,2304]{0,1:T(8,128)} %get-tuple-element.84) | copy-start | bytes 7077892
  546.3 24.3 %slice-start.7 = ((s8[4489216]{0:T(1024)(128)(4,1)}), s8[294912]{0:T(1024)(128)(4,1)S(1)}, s32[]{:S(2)}) async-start(s8[4489216]{0:T(1024)(128)(4,1)} %bitcast.227), calls=%async_computation.12 | async-start | bytes 589824
  590.1 12.6 copy-start.36
  590.1 12.6 copy-start.39
  602.7 9.4 copy-start.16
  612.1 10.5 copy-start.33
  613.5 9.1 copy-start.42
  613.5 9.1 copy-start.49
  613.5 9.1 copy-start.120
  639.1 863.7 %reduce-scatter.3.cloned.1.call-start = ((), (), s32[]{:S(2)}) async-start(), calls=%async_computation.3 | async-start | bytes 8454144 | tf_op jit(solution)/shard_map/reduce_scatter | solution.py:219
  (118 other events, 425.5 us)
Sparse Core Ops, SparseCore 0:
  9.7 200.8 all-gather.5
  212.3 203.7 all-gather.3
  639.2 219.1 all-reduce.38
  861.2 641.5 reduce-scatter.2
where the time goes:
time: 1530 us; the launch traced here: 1510 us
  waiting for transfers between devices  908 us (59%)
  blocking collectives  308 us (20%)
  matrix products  158 us (10%)
  other arithmetic  75.7 us (5%)
  local copies, waits for them, and re-layouts  43.4 us (3%)
  between operations  16.8 us (1%)
    reduce_scatter x1, waiting for transfers between devices, body(): lax.psum_scatter(weight_sums[5], ('dp', 'fsdp'), scatter_dimension=0, til...  643 us
    all_gather x1, blocking collectives, body(): lax.all_gather(shards[2], ('dp', 'fsdp'), axis=1, tiled=True)  174 us
    all_gather x1, waiting for transfers between devices, body(): lax.all_gather(shards[1], ('dp', 'fsdp'), axis=0, tiled=True)  149 us
    unnamed x2, blocking collectives  134 us
    unnamed x5, waiting for transfers between devices  116 us
    dot_general x6, matrix products, state_mix(): outputs = jnp.einsum('hts,shp->thp', mixing, values, precision=highest)  52.4 us
  transfers between devices with their start and end apart: 4, of which 3 were waited for; matrix products, arithmetic and copies ran while one was open for 3% of the time, Pallas kernels for 0%

commit v1 on v0

v1 whole, which is shorter than its diff:
```python
import jax
import jax.numpy as jnp
import numpy as np
from jax import lax
from jax.experimental import pallas as pl
from jax.experimental.pallas import tpu as pltpu
from jax.sharding import PartitionSpec as P

D = 1024
INNER = 2048
STATE = 128
HEAD = 64
CONV = 4
HEADS = 32
XBC = 2304
PROJ = 4384
TOK = 512
CHIPS = 64
COLS = 4608
SIDE = 3328
MESH = pl.DeviceIdType.MESH
ORDERS = (("x", "y", "z"), ("y", "z", "x"), ("z", "x", "y"))
OUT, GATE, REST = 0, 1, 2
EVEN = ((0, 384), (384, 384), (768, 256))
PARTS = {OUT: EVEN, GATE: EVEN, REST: ((0, 512), (512, 384), (896, 384))}
LOCAL = {OUT: 0, GATE: 1024, REST: 2048}
WIDTH = {GATE: 1024, REST: 1280}

eps = 1e-05
highest = lax.Precision.HIGHEST


def place():
    dp, fsdp = lax.axis_index("dp"), lax.axis_index("fsdp")
    return {"x": (fsdp // 2) % 4, "y": (dp // 4) * 2 + fsdp // 8, "z": dp % 4, "c": fsdp % 2}


def device(at):
    y = at["y"]
    return ((y // 2) * 4 + at["z"], (y % 2) * 8 + at["x"] * 2 + at["c"])


def moved(at, axis, step):
    size = 2 if axis == "c" else 4
    return dict(at, **{axis: lax.rem(at[axis] + step, size)})


def enter(at):
    barrier = pltpu.get_barrier_semaphore()
    peers = [moved(at, axis, step) for axis in "xyz" for step in (1, 2, 3)] + [moved(at, "c", 1)]
    for peer in peers:
        pl.semaphore_signal(barrier, inc=1, device_id=device(peer), device_id_type=MESH)
    pl.semaphore_wait(barrier, len(peers))


def remote(src, dst, send, recv, peer):
    return pltpu.make_async_remote_copy(
        src_ref=src, dst_ref=dst, send_sem=send, recv_sem=recv, device_id=device(peer), device_id_type=MESH
    )


def chips(at, full):
    every = slice(None)
    y, z, x = at["y"], at["z"], at["x"]
    return (
        every if "y" in full else y // 2,
        every if "z" in full else z,
        every if "y" in full else y % 2,
        every if "x" in full else x,
    )


def rolled_down(x, step):
    zeros = jnp.zeros((8, x.shape[1]), x.dtype)
    return pltpu.roll(jnp.concatenate([zeros, x], axis=0), step, axis=0)[8:]


def rolled_up(x, step):
    rows = x.shape[0]
    zeros = jnp.zeros((8, x.shape[1]), x.dtype)
    return pltpu.roll(jnp.concatenate([x, zeros], axis=0), rows + 8 - step, axis=0)[:rows]


def tile(j, base=0, size=128):
    return pl.ds(pl.multiple_of(base + j * size, 128), size)


def dot_nt(a, b):
    return lax.dot_general(a, b, (((1,), (1,)), ((), ())), preferred_element_type=jnp.float32)


def dot(a, b, **more):
    return jnp.dot(a, b, preferred_element_type=jnp.float32, **more)


def row_sum(x):
    return jnp.sum(x, axis=1, keepdims=True)


def col_sum(x):
    return jnp.sum(x, axis=0, keepdims=True)


def block_kernel(
    wi,
    wo,
    tokens,
    cotangent,
    live,
    heads,
    skip,
    spots,
    block_out,
    input_grad,
    gi_out,
    go_out,
    small_out,
    full_in,
    other,
    blk,
    full_out,
    work,
    proj,
    act,
    dsilu,
    y_ref,
    dinner,
    dproj,
    inner_t,
    normed,
    normed_t,
    mix,
    mix_t,
    cum_ref,
    cum_t,
    step_ref,
    q_ref,
    m_ref,
    dcum_ref,
    dstep_ref,
    taps,
    gain,
    norm_gain,
    part0,
    recv1,
    part1,
    recv2,
    part2,
    recv3,
    swap_from,
    swap_to,
    small_now,
    small_got,
    swap_sem,
    local_sem,
    ag_send,
    ag_recv,
    ag_pass,
    ag_got,
    rs_send,
    rs_recv,
    rs_pass,
    rs_got,
    small_send,
    small_recv,
):
    low, full = jnp.bfloat16, jnp.float32
    at = place()
    core = at["c"]
    first = core == 0
    sibling = moved(at, "c", 1)
    here = chips(at, ())
    enter(at)

    swap = remote(wi, other, swap_sem.at[0], swap_sem.at[1], sibling)
    swap.start()
    full_out[here + (core,)] = wo[...]

    def held(batch, part, reach):
        start, width = PARTS[batch][part]
        if batch == OUT:
            return full_out.at[chips(at, reach) + (core, slice(None), pl.ds(start, width))]
        column = core * WIDTH[batch] + start + (INNER if batch == REST else 0)
        return full_in.at[chips(at, reach) + (slice(None), pl.ds(pl.multiple_of(column, 128), width))]

    flying = {}
    drained = []

    def hop(batch, part, phase):
        target = held(batch, part, ORDERS[part][:phase])
        source = target
        if phase == 0 and batch != OUT:
            start, width = PARTS[batch][part]
            source = blk.at[:, pl.ds((INNER // 2 if batch == REST else 0) + start, width)]
        flying[batch, part] = []
        for step in (1, 2, 3):
            slot = ((batch * 3 + part) * 3 + phase) * 3 + step - 1
            copy = remote(source, target, ag_send.at[slot], ag_recv.at[slot], moved(at, ORDERS[part][phase], step))
            copy.start()
            flying[batch, part].append(copy)
            drained.append(copy)

    def landed(batch, part):
        for copy in flying[batch, part]:
            copy.wait_recv()

    given = {}

    def give(batch):
        for part in range(3):
            landed(batch, part)
            region = held(batch, part, "xyz")
            slot = batch * 3 + part
            given[batch, part] = remote(region, region, ag_pass.at[slot], ag_got.at[slot], sibling)
            given[batch, part].start()
            drained.append(given[batch, part])

    def taken(batch):
        for part in range(3):
            given[batch, part].wait_recv()

    swap.wait()
    for batch, base in ((GATE, 0), (REST, INNER)):
        width = WIDTH[batch]
        lanes = pl.ds(pl.multiple_of(base + core * width, 128), width)
        mine, theirs = wi[:, lanes], other[:, lanes]
        blk[:, base // 2 : base // 2 + width] = jnp.concatenate(
            [jnp.where(first, mine, theirs), jnp.where(first, theirs, mine)], axis=0
        ).astype(low)
    stores = []
    for batch, base in ((REST, INNER), (GATE, 0)):
        width = WIDTH[batch]
        lanes = pl.ds(pl.multiple_of(base + core * width, 128), width)
        copy = pltpu.make_async_copy(
            blk.at[:, pl.ds(base // 2, width)], full_in.at[here + (slice(None), lanes)], local_sem.at[len(stores)]
        )
        copy.start()
        stores.append(copy)
    for batch in (REST, GATE, OUT):
        for part in range(3):
            hop(batch, part, 0)
    for copy in stores:
        copy.wait()
    for phase in (1, 2):
        for batch in (REST, GATE, OUT):
            for part in range(3):
                landed(batch, part)
                hop(batch, part, phase)

    lane = lax.broadcasted_iota(jnp.int32, (TOK, 128), 1)
    left = lane < HEAD
    row = lax.broadcasted_iota(jnp.int32, (TOK, TOK), 0)
    column = lax.broadcasted_iota(jnp.int32, (TOK, TOK), 1)
    m_ref[...] = jnp.zeros_like(m_ref)
    for j in range(D // 128):
        x = tokens[:, j * 128 : j * 128 + 128].astype(full)
        m_ref[...] += x * x
    token_scale = lax.rsqrt(row_sum(m_ref[...]) / D + eps)

    def loaded(slot, column, width):
        return pltpu.make_async_copy(
            full_in.at[:, :, :, :, :, pl.ds(column, width)],
            work.reshape(4, 4, 2, 4, 16, 512).at[pl.ds(2 * slot, 2), :, :, :, :, pl.ds(0, width)],
            local_sem.at[2 + slot],
        )

    def streamed(columns, use):
        copies = [loaded(i % 2, column, width) for i, (column, width) in enumerate(columns)]
        copies[0].start()
        for i, (column, width) in enumerate(columns):
            if i + 1 < len(columns):
                copies[i + 1].start()
            copies[i].wait()
            use(column, width, work[pl.ds(CHIPS * (i % 2), CHIPS), :, :width].reshape(D, width))

    give(REST)
    taken(REST)
    load = loaded(1, COLS - 128, 128)
    load.start()
    load.wait()
    packed = work[CHIPS:, :, :128].reshape(D, 128)
    pick = lax.broadcasted_iota(jnp.int32, (128, D), 0) * 8 == lax.broadcasted_iota(jnp.int32, (128, D), 1)
    shared = dot(pick.astype(low), packed).astype(low)

    def spread(base, lanes, owners):
        count = lanes.shape[1]
        line = lax.broadcasted_iota(jnp.int32, (128, count), 0)
        found = dot(shared, (line == lanes + base).astype(low))
        return col_sum(jnp.where(line == owners, found, 0.0))

    count = lax.broadcasted_iota(jnp.int32, (1, INNER), 1)
    norm_gain[...] = spread(0, count[:, :D] & 7, count[:, :D] >> 3)
    gain[...] = spread(8, count & 15, count >> 4)
    taps[...] = jnp.zeros_like(taps)
    taps[4:5, :] = spread(24, spots[0:1, :], spots[1:2, :])
    for k in range(CONV):
        taps[k : k + 1, :] = spread(42 + 18 * k, spots[0:1, :], spots[1:2, :])

    for j in range(D // 128):
        cols = slice(j * 128, j * 128 + 128)
        value = (tokens[:, cols].astype(full) * token_scale * norm_gain[:, cols]).astype(low)
        normed[:, cols] = value
        normed_t[j * 8 : j * 8 + 8] = value.T.reshape(8, 16, TOK)

    def project(column, width, weight):
        proj[:, column : column + width] = dot(normed[...], weight)

    streamed([(INNER + 512 * i, 512) for i in range(4)] + [(COLS - 512, 384)], project)
    give(GATE)

    @pl.loop(0, XBC // 128)
    def _(j):
        cols = tile(j)
        x = proj[:, tile(j, INNER)]
        pre = taps[4:5, cols] + taps[3:4, cols] * x
        for step in (1, 2, 3):
            pre = pre + taps[3 - step : 4 - step, cols] * rolled_down(x, step)
        sig = jax.nn.sigmoid(pre)
        act[:, cols] = (pre * sig).astype(low)
        dsilu[:, cols] = (sig * (1.0 + pre * (1.0 - sig))).astype(low)

    raw = proj[:, INNER + XBC : INNER + XBC + 128] + heads[0:1, :]
    grown = jnp.exp(-jnp.abs(raw))
    more = 1.0 + grown
    logged = jnp.where(more == 1.0, grown, jnp.log(more) * grown / jnp.where(more == 1.0, 1.0, more - 1.0))
    steps = jnp.where(lane < HEADS, jnp.maximum(raw, 0.0) + logged, 0.0)
    rate = -jnp.exp(heads[1:2, :])
    cum = dot((row >= column).astype(full), steps * rate, precision=highest)
    step_ref[...] = steps
    cum_ref[...] = cum
    turned = cum.T
    for head in range(HEADS):
        cum_t[head] = turned[head : head + 1]
    mixed = jnp.where(row >= column, dot_nt(act[:, INNER + STATE :], act[:, INNER : INNER + STATE]), 0.0)
    mix[...] = mixed
    mix_t[...] = mixed.T

    taken(GATE)
    streamed([(512 * i, 512) for i in range(4)], project)
    give(OUT)
    q_ref[...] = jnp.zeros_like(q_ref)
    dcum_ref[...] = jnp.zeros_like(dcum_ref)
    dstep_ref[...] = jnp.zeros_like(dstep_ref)

    def pair(j):
        turn = lax.rem(128 - 2 * j, 128)
        cums = pltpu.roll(cum_ref[...], turn, axis=1)
        sizes = pltpu.roll(step_ref[...], turn, axis=1)
        wide = jnp.where(left, sizes[:, 0:1], sizes[:, 1:2])
        values = act[:, tile(j)].astype(full)
        return cums, wide, values, (values * wide).astype(low)

    @pl.loop(0, HEADS // 2)
    def _(j):
        cols = tile(j)
        cums, _, values, scaled = pair(j)
        for block in range(TOK // 128):
            start, last = block * 128, block * 128 + 128
            found = []
            for e in (0, 1):
                pieces = []
                for past in range(block + 1):
                    span = slice(past * 128, past * 128 + 128)
                    gap = cums[start:last, e : e + 1] - cum_t[2 * j + e, :, span]
                    if past == block:
                        gap = jnp.minimum(gap, 0.0)
                    pieces.append((mix[start:last, span] * jnp.exp(gap)).astype(low))
                found.append(dot(jnp.concatenate(pieces, axis=1), scaled[:last]))
            y = jnp.where(left[:128], found[0], found[1]) + skip[:, cols] * values[start:last]
            y_ref[start:last, cols] = y
            gate = proj[start:last, cols]
            gated = y * gate * jax.nn.sigmoid(gate)
            q_ref[start:last] += gated * gated

    q_ref[...] = jnp.broadcast_to(lax.rsqrt(row_sum(q_ref[...]) / INNER + eps), (TOK, 128))
    mix[...] = jnp.zeros_like(mix)

    @pl.loop(0, INNER // 128)
    def _(j):
        cols = tile(j)
        gate = proj[:, cols]
        gated = y_ref[:, cols] * gate * jax.nn.sigmoid(gate)
        value = (gated * q_ref[...] * gain[:, cols]).astype(low)
        dproj[:, cols] = value
        inner_t[pl.ds(4 * j, 4)] = value.T.reshape(4, 2, 16, TOK)

    for j in range(D // 128):
        cols = slice(j * 128, j * 128 + 128)
        normed[:, cols] = (live[...] * cotangent[:, cols].astype(full)).astype(low)

    def grads(batch, part, side, half):
        start, width = PARTS[batch][part]
        if batch == OUT:
            lhs = inner_t[pl.ds(32 * half, 32), side].reshape(TOK, TOK)
            rhs = normed[:, start : start + width]
        else:
            lhs = normed_t[pl.ds(32 * half, 32)].reshape(TOK, TOK)
            base = (INNER if batch == REST else 0) + start
            rhs = dproj[:, pl.ds(pl.multiple_of(base + side * WIDTH[batch], 128), width)]
        return dot(lhs, rhs)

    def spot_of(part, half, m):
        spot = {"y": 2 * half + (m // 4) % 2, "z": m // 8, "x": m % 4}
        axes = ORDERS[part]
        return spot[axes[2]] * 16 + spot[axes[1]] * 4 + spot[axes[0]]

    users = [None, None]

    def rs_give(batch, part, slot):
        if users[slot] is not None:
            users[slot].wait_send()
        width = PARTS[batch][part][1]
        for half in (0, 1):
            value = grads(batch, part, 1 - core, half).astype(low)
            for m in range(32):
                work[CHIPS * slot + spot_of(part, half, m), :, :width] = value[16 * m : 16 * m + 16]
        copy = rs_pass_copy(batch, part, slot)
        copy.start()
        users[slot] = copy

    def rs_pass_copy(batch, part, slot):
        width = PARTS[batch][part][1]
        sem = batch * 3 + part
        return remote(
            work.at[pl.ds(CHIPS * slot, CHIPS), :, pl.ds(0, width)],
            part0.at[:, :, lanes_of(batch, part)],
            rs_pass.at[sem],
            rs_got.at[sem],
            sibling,
        )

    def lanes_of(batch, part):
        start, width = PARTS[batch][part]
        return pl.ds(LOCAL[batch] + start, width)

    def rs_copies(batch, part, stage):
        lanes = lanes_of(batch, part)
        axis = ORDERS[part][3 - stage]
        copies = []
        for step in (1, 2, 3):
            peer = moved(at, axis, step)
            there, slot = peer[axis], pl.ds(step - 1, 1)
            if stage == 1:
                source, target = part0.at[pl.ds(there * 16, 16), :, lanes], recv1.at[pl.ds(16 * step - 16, 16), :, lanes]
            elif stage == 2:
                source, target = part1.at[pl.ds(there * 4, 4), :, lanes], recv2.at[pl.ds(4 * step - 4, 4), :, lanes]
            else:
                source, target = part2.at[pl.ds(there, 1), :, lanes], recv3.at[slot, :, lanes]
            sem = ((batch * 3 + part) * 3 + stage - 1) * 3 + step - 1
            copies.append(remote(source, target, rs_send.at[sem], rs_recv.at[sem], peer))
        return copies

    def rs_hop(batch, part, stage):
        for copy in rs_copies(batch, part, stage):
            copy.start()

    def rs_landed(batch, part, stage):
        for copy in rs_copies(batch, part, stage):
            copy.wait_recv()

    def rs_own(batch, part):
        lanes = lanes_of(batch, part)
        rs_pass_copy(batch, part, 0).wait_recv()
        for half in (0, 1):
            value = grads(batch, part, core, half)
            for m in range(32):
                spot = spot_of(part, half, m)
                now = pl.ds(spot, 1)
                part0[now, :, lanes] = (value[16 * m : 16 * m + 16][None] + part0[now, :, lanes].astype(full)).astype(low)
        rs_hop(batch, part, 1)

    def rs_one(batch, part):
        lanes = lanes_of(batch, part)
        rs_landed(batch, part, 1)
        mine = at[ORDERS[part][2]] * 16
        for i in range(16):
            now = pl.ds(i, 1)
            value = part0[pl.ds(mine + i, 1), :, lanes].astype(full)
            for k in range(3):
                value = value + recv1[pl.ds(16 * k + i, 1), :, lanes].astype(full)
            part1[now, :, lanes] = value.astype(low)
        rs_hop(batch, part, 2)

    def rs_two(batch, part):
        lanes = lanes_of(batch, part)
        rs_landed(batch, part, 2)
        mine = at[ORDERS[part][1]] * 4
        for i in range(4):
            now = pl.ds(i, 1)
            value = part1[pl.ds(mine + i, 1), :, lanes].astype(full)
            for k in range(3):
                value = value + recv2[pl.ds(4 * k + i, 1), :, lanes].astype(full)
            part2[now, :, lanes] = value.astype(low)
        rs_hop(batch, part, 3)

    def rs_three(batch, part):
        lanes = lanes_of(batch, part)
        rs_landed(batch, part, 3)
        value = part2[pl.ds(at[ORDERS[part][0]], 1), :, lanes].astype(full)
        for k in range(3):
            value = value + recv3[pl.ds(k, 1), :, lanes].astype(full)
        value = value[0]
        start, width = PARTS[batch][part]
        if batch == OUT:
            go_out[:, start : start + width] = value
            return
        base = INNER if batch == REST else 0
        at_column = pl.multiple_of(base + core * WIDTH[batch] + start, 128)
        gi_out[:, pl.ds(at_column, width)] = jnp.where(first, value[:8], value[8:])
        swap_from[:, pl.ds(base // 2 + start, width)] = jnp.where(first, value[8:], value[:8])

    taken(OUT)
    wout = full_out.reshape(INNER, D)
    for part in range(2):
        rs_give(OUT, part, part)

    wide_live = jnp.concatenate([live[...], live[...]], axis=1)

    @pl.loop(0, D // 256)
    def _(j):
        cols = tile(j, 0, 256)
        branch = dot(dproj[:, :INNER], wout[:, cols])
        block_out[:, cols] = (tokens[:, cols].astype(full) + wide_live * branch).astype(low)

    rs_give(OUT, 2, 0)

    @pl.loop(0, INNER // 256)
    def _(j):
        cols = tile(j, 0, 256)
        dinner[:, cols] = dot_nt(normed[...], wout[cols, :])

    m_ref[...] = jnp.zeros_like(m_ref)

    @pl.loop(0, INNER // 128)
    def _(j):
        cols = tile(j)
        gate = proj[:, cols]
        u = y_ref[:, cols] * gate * jax.nn.sigmoid(gate) * q_ref[...]
        du = dinner[:, cols] * u
        small_now[0, 5:6, cols] = col_sum(du)
        m_ref[...] += du * gain[:, cols]

    m_ref[...] = jnp.broadcast_to(row_sum(m_ref[...]) / INNER, (TOK, 128))

    @pl.loop(0, INNER // 128)
    def _(j):
        cols = tile(j)
        y, gate, q = y_ref[:, cols], proj[:, cols], q_ref[...]
        sig = jax.nn.sigmoid(gate)
        silu = gate * sig
        dgated = q * (dinner[:, cols] * gain[:, cols] - y * silu * q * m_ref[...])
        dproj[:, cols] = (dgated * y * sig * (1.0 + gate * (1.0 - sig))).astype(low)
        dinner[:, cols] = dgated * silu

    rs_give(GATE, 0, 1)
    for part in range(3):
        rs_own(OUT, part)
    rs_give(GATE, 1, 0)
    rs_give(GATE, 2, 1)

    def conv_back(dact, j):
        cols = tile(j)
        x = proj[:, tile(j, INNER)]
        dpre = dact * dsilu[:, cols].astype(full)
        small_now[0, 4:5, cols] = col_sum(dpre)
        small_now[0, 3:4, cols] = col_sum(dpre * x)
        dx = taps[3:4, cols] * dpre
        for step in (1, 2, 3):
            moved_up = rolled_up(dpre, step)
            small_now[0, 3 - step : 4 - step, cols] = col_sum(moved_up * x)
            dx = dx + taps[3 - step : 4 - step, cols] * moved_up
        dproj[:, tile(j, INNER)] = dx.astype(low)

    @pl.loop(0, HEADS // 2)
    def _(j):
        for turn, work_now in (
            (2, lambda part: rs_own(GATE, part)),
            (5, lambda part: rs_one(OUT, part)),
            (8, lambda part: rs_one(GATE, part)),
            (10, lambda part: rs_two(OUT, part)),
            (12, lambda part: rs_two(GATE, part)),
            (14, lambda part: rs_three(OUT, part)),
        ):

            @pl.when(j == turn)
            def _(work_now=work_now):
                for part in range(3):
                    work_now(part)

        cols = tile(j)
        cums, wide, values, scaled = pair(j)
        y, dy = y_ref[:, cols], dinner[:, cols]
        dy_low = dy.astype(low)
        small_now[0, 7:8, cols] = col_sum(dy * values)
        own = (jnp.where(left, scaled, jnp.zeros_like(scaled)), jnp.where(left, jnp.zeros_like(scaled), scaled))
        found = []
        for block in range(TOK // 128):
            start, last = block * 128, block * 128 + 128
            both = []
            total = None
            for e in (0, 1):
                dm = dot_nt(own[e][start:last], dy_low[start:])
                pieces, shares = [], []
                for later in range(block, TOK // 128):
                    span = slice(later * 128, later * 128 + 128)
                    gap = cum_t[2 * j + e, :, span] - cums[start:last, e : e + 1]
                    if later == block:
                        gap = jnp.minimum(gap, 0.0)
                    decay = jnp.exp(gap)
                    pieces.append((mix_t[start:last, span] * decay).astype(low))
                    shares.append(dm[:, (later - block) * 128 : (later - block + 1) * 128] * decay)
                both.append(dot(jnp.concatenate(pieces, axis=1), dy_low[start:]))
                share = jnp.concatenate(shares, axis=1)
                total = share if total is None else total + share
            mix[start:last, start:] += total
            found.append(jnp.where(left[:128], both[0], both[1]))
        back = jnp.concatenate(found, axis=0)
        direct = values * back
        crossing = dy_low.astype(full) * (y - skip[:, cols] * values) - scaled.astype(full) * back
        for e in (0, 1):
            mine = left if e == 0 else jnp.logical_not(left)
            spot = lane == 2 * j + e
            dcum_ref[...] = jnp.where(spot, row_sum(jnp.where(mine, crossing, 0.0)), dcum_ref[...])
            dstep_ref[...] = jnp.where(spot, row_sum(jnp.where(mine, direct, 0.0)), dstep_ref[...])
        conv_back(wide * back + skip[:, cols] * dy, j)

    masked = jnp.where(row <= column, mix[...], 0.0)
    conv_back(dot(masked.astype(low), act[:, INNER + STATE :]), INNER // 128)
    conv_back(dot(masked.T.astype(low), act[:, INNER : INNER + STATE]), INNER // 128 + 1)
    dacc = dot((row <= column).astype(full), dcum_ref[...], precision=highest)
    dstep = dstep_ref[...] + dacc * rate
    draw = jnp.where(
        lane < HEADS, dstep * jax.nn.sigmoid(proj[:, INNER + XBC : INNER + XBC + 128] + heads[0:1, :]), 0.0
    )
    dproj[:, INNER + XBC : INNER + XBC + 128] = draw.astype(low)
    dproj[:, INNER + XBC + 128 :] = jnp.zeros((TOK, 128), low)
    small_now[0, 6:7, :] = jnp.zeros((1, XBC), full)
    small_now[0, 6:7, D : D + 128] = col_sum(draw)
    small_now[0, 6:7, D + 128 : D + 256] = rate * col_sum(dacc * step_ref[...])
    small_now[0, 5:6, INNER:] = jnp.zeros((1, XBC - INNER), full)
    small_now[0, 7:8, INNER:] = jnp.zeros((1, XBC - INNER), full)

    rs_give(REST, 0, 0)
    rs_give(REST, 1, 1)
    for part in range(3):
        rs_three(GATE, part)
    rs_give(REST, 2, 0)
    for part in range(3):
        rs_own(REST, part)

    for slot in (0, 1):
        users[slot].wait_send()
    dnormed = y_ref.at[:, pl.ds(0, D)]
    dnormed[...] = jnp.zeros((TOK, D), full)

    def unproject(column, width, weight):
        dnormed[...] += dot_nt(dproj[:, column : column + width], weight)

    streamed([(512 * i, 512) for i in range(9)], unproject)
    m_ref[...] = jnp.zeros_like(m_ref)
    for j in range(D // 128):
        cols = slice(j * 128, j * 128 + 128)
        u = tokens[:, cols].astype(full) * token_scale
        du = dnormed[:, cols] * u
        small_now[0, 6:7, cols] = col_sum(du)
        m_ref[...] += du * norm_gain[:, cols]
    mean = row_sum(m_ref[...]) / D

    small_copies = [[], [], [], []]

    def small_start(stage):
        for step in (1,) if stage == 0 else (1, 2, 3):
            slot = 0 if stage == 0 else stage * 3 - 3 + step
            copy = remote(
                small_now.at[stage],
                small_got.at[slot],
                small_send.at[slot],
                small_recv.at[slot],
                moved(at, "cxyz"[stage], step),
            )
            copy.start()
            small_copies[stage].append((slot, copy))
            drained.append(copy)

    def small_sum(stage):
        value = small_now[stage]
        for slot, copy in small_copies[stage]:
            copy.wait_recv()
            value = value + small_got[slot]
        if stage < 3:
            small_now[stage + 1] = value
            small_start(stage + 1)
        else:
            small_out[...] = value

    small_start(0)
    for part in range(3):
        rs_one(REST, part)
    for j in range(D // 128):
        cols = slice(j * 128, j * 128 + 128)
        u = tokens[:, cols].astype(full) * token_scale
        du = dnormed[:, cols] * norm_gain[:, cols]
        normed[:, cols] = (cotangent[:, cols].astype(full) + token_scale * (du - u * mean)).astype(low)
    final = pltpu.make_async_copy(normed, input_grad, local_sem.at[0])
    final.start()
    small_sum(0)
    for part in range(3):
        rs_two(REST, part)
    small_sum(1)
    for part in range(3):
        rs_three(REST, part)
    last = remote(swap_from, swap_to, swap_sem.at[2], swap_sem.at[3], sibling)
    last.start()
    small_sum(2)
    for copy in drained:
        copy.wait_send()
    for batch in (OUT, GATE, REST):
        for part in range(3):
            for stage in (1, 2, 3):
                for copy in rs_copies(batch, part, stage):
                    copy.wait_send()
    last.wait()
    for base, width in ((0, WIDTH[GATE]), (INNER, WIDTH[REST])):
        lanes = pl.ds(pl.multiple_of(base + (1 - core) * width, 128), width)
        gi_out[:, lanes] = swap_to[:, base // 2 : base // 2 + width]
    final.wait()
    small_sum(3)


def block(wi, wo, tokens, cotangent, live, heads, skip, spots):
    full, low = jnp.float32, jnp.bfloat16
    vmem, anywhere = pl.BlockSpec(memory_space=pltpu.VMEM), pl.BlockSpec(memory_space=pl.ANY)
    sems = pltpu.SemaphoreType.DMA
    return pl.pallas_call(
        block_kernel,
        out_shape=(
            jax.ShapeDtypeStruct((TOK, D), low),
            jax.ShapeDtypeStruct((TOK, D), low),
            jax.ShapeDtypeStruct((8, COLS), full),
            jax.ShapeDtypeStruct((16, D), full),
            jax.ShapeDtypeStruct((8, XBC), full),
            jax.ShapeDtypeStruct((2, 4, 2, 4, 16, COLS), low),
        ),
        in_specs=[vmem] * 8,
        out_specs=[vmem, anywhere] + [vmem] * 3 + [anywhere],
        scratch_shapes=[
            pltpu.VMEM((8, COLS), full),
            pltpu.VMEM((16, XBC), low),
            pltpu.VMEM((2, 4, 2, 4, 2, 16, D), low),
            pltpu.VMEM((2 * CHIPS, 16, 512), low),
            pltpu.VMEM((TOK, COLS - 128), full),
            pltpu.VMEM((TOK, XBC), low),
            pltpu.VMEM((TOK, XBC), low),
            pltpu.VMEM((TOK, INNER), full),
            pltpu.VMEM((TOK, INNER), full),
            pltpu.VMEM((TOK, COLS), low),
            pltpu.VMEM((CHIPS, 2, 16, TOK), low),
            pltpu.VMEM((TOK, D), low),
            pltpu.VMEM((CHIPS, 16, TOK), low),
            pltpu.VMEM((TOK, TOK), full),
            pltpu.VMEM((TOK, TOK), full),
            pltpu.VMEM((TOK, 128), full),
            pltpu.VMEM((HEADS, 1, TOK), full),
            pltpu.VMEM((TOK, 128), full),
            pltpu.VMEM((TOK, 128), full),
            pltpu.VMEM((TOK, 128), full),
            pltpu.VMEM((TOK, 128), full),
            pltpu.VMEM((TOK, 128), full),
            pltpu.VMEM((8, XBC), full),
            pltpu.VMEM((1, INNER), full),
            pltpu.VMEM((1, D), full),
            pltpu.VMEM((CHIPS, 16, SIDE), low),
            pltpu.VMEM((48, 16, SIDE), low),
            pltpu.VMEM((16, 16, SIDE), low),
            pltpu.VMEM((12, 16, SIDE), low),
            pltpu.VMEM((4, 16, SIDE), low),
            pltpu.VMEM((3, 16, SIDE), low),
            pltpu.VMEM((8, XBC), full),
            pltpu.VMEM((8, XBC), full),
            pltpu.VMEM((4, 8, XBC), full),
            pltpu.VMEM((10, 8, XBC), full),
            sems((4,)),
            sems((4,)),
            sems((81,)),
            sems((81,)),
            sems((9,)),
            sems((9,)),
            sems((81,)),
            sems((81,)),
            sems((9,)),
            sems((9,)),
            sems((10,)),
            sems((10,)),
        ],
        compiler_params=pltpu.CompilerParams(collective_id=0, has_side_effects=True, vmem_limit_bytes=63 << 20),
    )(wi, wo, tokens, cotangent, live, heads, skip, spots)


def body(
    tokens,
    lengths,
    placement_ids,
    norm_gain,
    in_weight,
    conv_weight,
    conv_bias,
    dt_bias,
    a_log,
    d_skip,
    inner_gain,
    out_weight,
    cotangent,
):
    full = jnp.float32
    sequence_id = placement_ids[0]
    slot_length = jnp.sum(jnp.where(lax.broadcasted_iota(jnp.int32, lengths.shape, 0) == sequence_id, lengths, 0))
    live = (lax.broadcasted_iota(jnp.int32, (TOK, 128), 0) < slot_length).astype(full)
    shared = jnp.concatenate(
        [norm_gain, inner_gain, conv_bias, conv_weight.reshape(-1), jnp.zeros((14,), jnp.bfloat16)]
    )
    wi = jnp.concatenate(
        [
            in_weight,
            jnp.zeros((8, COLS - 128 - PROJ), jnp.bfloat16),
            jnp.pad(shared[None], ((0, 7), (0, 0))),
        ],
        axis=1,
    ).astype(full)
    heads = jnp.pad(jnp.stack([dt_bias, a_log]), ((0, 6), (0, 128 - HEADS)))
    count = np.arange(XBC, dtype=np.int32)
    spots = jnp.asarray(np.stack([count % 18, count // 18] + [count * 0] * 6))
    block_out, input_grad, shard_in, shard_out, small, _ = block(
        wi, out_weight, tokens, cotangent, live, heads, jnp.repeat(d_skip, HEAD)[None], spots
    )
    me = lax.axis_index("dp") * 16 + lax.axis_index("fsdp")
    conv = lax.dynamic_slice(small, (0, me * 18), (5, 18))
    return (
        block_out,
        input_grad,
        lax.dynamic_slice(small, (6, me * 8), (1, 8))[0],
        shard_in[:, :PROJ],
        conv[:CONV],
        conv[CONV],
        small[6, D : D + HEADS],
        small[6, D + 128 : D + 128 + HEADS],
        jnp.sum(small[7, :INNER].reshape(HEADS, HEAD), axis=1),
        lax.dynamic_slice(small, (5, me * 16), (1, 16))[0],
        shard_out,
    )


def solution(mesh):
    placed = (
        P(("dp", "fsdp"), None),
        P(),
        P(("dp", "fsdp")),
        P(("dp", "fsdp")),
        P(("dp", "fsdp"), None),
        P(None, ("dp", "fsdp")),
        P(("dp", "fsdp")),
        P(),
        P(),
        P(),
        P(("dp", "fsdp")),
        P(("dp", "fsdp"), None),
        P(("dp", "fsdp"), None),
    )
    return jax.shard_map(
        body,
        mesh=mesh,
        in_specs=placed,
        out_specs=(
            P(("dp", "fsdp"), None),
            P(("dp", "fsdp"), None),
            P(("dp", "fsdp")),
            P(("dp", "fsdp"), None),
            P(None, ("dp", "fsdp")),
            P(("dp", "fsdp")),
            P(),
            P(),
            P(),
            P(("dp", "fsdp")),
            P(("dp", "fsdp"), None),
        ),
        check_vma=False,
    )
```

time: 1530 us -> 195 us (0.13); the launches traced: 1510 us -> 192 us
  waiting for transfers between devices: 908 us -> 0 us
  blocking collectives: 308 us -> 0 us
  Pallas kernels: 0 us -> 166 us
  matrix products: 158 us -> 0 us
  other arithmetic: 75.7 us -> 4.52 us
  local copies, waits for them, and re-layouts: 43.4 us -> 20.2 us
  between operations: 16.8 us -> 1.33 us
    reduce_scatter x1 -> x0, waiting for transfers between devices: 643 us -> none  [body(): lax.psum_scatter(weight_sums[5], ('dp', 'fsdp'), scatter_dimension=0, til...]
    all_gather x1 -> x0, blocking collectives: 174 us -> none  [body(): lax.all_gather(shards[2], ('dp', 'fsdp'), axis=1, tiled=True)]
    pallas_call x0 -> x1, Pallas kernels: none -> 166 us  [block(): pl.pallas_call(block_kernel, out_shape=(jax.ShapeDtypeStruct((TOK, D), lo...]
    dot_general x34 -> x0, matrix products: 158 us -> none  [the longest x6 52.4 us: state_mix(): outputs = jnp.einsum('hts,shp->thp', mixing, values, precision=highest)]
    all_gather x2 -> x0, waiting for transfers between devices: 149 us -> none  [the longest x1 149 us: body(): lax.all_gather(shards[1], ('dp', 'fsdp'), axis=0, tiled=True)]
    unnamed x2 -> x0, blocking collectives: 134 us -> none
    unnamed x5 -> x0, waiting for transfers between devices: 116 us -> none
    reduce_sum x12 -> x1, other arithmetic: 28.3 us -> 0.63 us  [body(): jnp.sum(small[7, :INNER].reshape(HEADS, HEAD), axis=1)]
  transfers between devices with their start and end apart: 4 -> 0, of which waited for: 3 -> 0; matrix products, arithmetic and copies ran while one was open for 3% -> 0% of each run, Pallas kernels for 0% -> 0%
where the time goes in v1:
time: 195 us; the launch traced here: 192 us
  Pallas kernels  166 us (85%)
  local copies, waits for them, and re-layouts  20.2 us (10%)
  other arithmetic  4.52 us (2%)
    pallas_call x1, Pallas kernels, block(): pl.pallas_call(block_kernel, out_shape=(jax.ShapeDtypeStruct((TOK, D), lo...  166 us
    unnamed x3, local copies, waits for them, and re-layouts  6 us

profile of v1, /device:TPU:1, one launch (start us, length us, event | category | flops | bytes accessed | tf_op | source)
XLA Modules:
  0.0 192.4 jit_solution(3402701643701043690)
XLA Ops:
  0.6 0.8 reshape.25
  1.4 2.1 %concatenate.6 = bf16[128]{0:T(256)(128)(2,1)S(1)} concatenate(bf16[8]{0:T(256)(128)(2,1)} %param.17, bf16[16]{0:T(256)(128)(2,1)} %param.24, bf16[18]{0:T(256)(128)(2,1)} %param.20, bf16[72]{0:T(256)(128)(2,1)S(1)} %reshape.25, bf16[14]{0:T(256)(128)(2,1)S(1)} %broadcast.10), dimensions={0} | concatenate | bytes 512 | tf_op jit(solution)/shard_map/concatenate | solution.py:818
  3.5 1.0 concatenate.7
  4.5 0.7 convert_element_type.10.wi
  5.8 1.3 fusion.1
  7.1 0.6 fusion
  7.8 0.8 iota.11.live
  8.6 1.3 select_maximum_fusion.heads
  9.9 0.7 broadcast_in_dim.16
  10.6 0.7 broadcast_in_dim_reshape.3.skip
  11.3 166.4 %shard_map.221 = (bf16[512,1024]{1,0:T(8,128)(2,1)}, bf16[512,1024]{1,0:T(8,128)(2,1)}, f32[8,4608]{1,0:T(8,128)}, f32[16,1024]{1,0:T(8,128)}, f32[8,2304]{1,0:T...) custom-call(f32[8,4608]{1,0:T(8,128)} %convert_element_type.10.wi, bf16[16,1024]{1,0:T(8,128)(2,1)} %wo.1, ...), custom_call_target="tpu_custom_call" | custom-call | tf_op jit(solution)/shard_map/pallas_call | solution.py:734
  177.7 1.3 dynamic-slice_bitcast_fusion.1
  179.0 1.6 slice.18
  180.5 0.8 constant_dynamic-slice_fusion
  181.3 0.6 slice.19
  181.9 0.5 slice_bitcast_fusion.2
  182.4 1.2 slice_bitcast_fusion
  183.6 0.9 slice_reduce_fusion
  184.5 0.1 reshape_squeeze.3
  184.6 0.6 reduce_sum.19
  185.2 1.3 dynamic-slice_bitcast_fusion
  186.4 2.3 %copy.29 = bf16[512,1024]{1,0:T(8,128)(2,1)} copy(bf16[512,1024]{1,0:T(8,128)(2,1)} %get-tuple-element.34) | data formatting | bytes 2097152
  188.7 2.3 %copy.30 = bf16[512,1024]{1,0:T(8,128)(2,1)} copy(bf16[512,1024]{1,0:T(8,128)(2,1)} %get-tuple-element.35) | data formatting | bytes 2097152
  191.0 1.5 copy.31
  (3 shorter events, 0.0 us)

commit v2 on v1

v2 whole, which is shorter than its diff:
```python
import jax
import jax.numpy as jnp
import numpy as np
from jax import lax
from jax.experimental import pallas as pl
from jax.experimental.pallas import tpu as pltpu
from jax.sharding import PartitionSpec as P

D = 1024
INNER = 2048
STATE = 128
HEAD = 64
CONV = 4
HEADS = 32
XBC = 2304
PROJ = 4384
TOK = 512
CHIPS = 64
COLS = 4608
SIDE = 3328
HALF = 1152
THIRD = 384
MESH = pl.DeviceIdType.MESH
ORDERS = (("x", "y", "z"), ("y", "z", "x"), ("z", "x", "y"))
OUT, GATE, EARLY, LATE = 0, 1, 2, 3
PARTS = {
    OUT: ((0, 512), (512, 256), (768, 256)),
    GATE: ((0, 256), (256, 256), (512, 512)),
    EARLY: ((0, 256), (256, 256), (512, 256)),
    LATE: ((0, 128), (128, 256), (384, 128)),
}
GROUPS = {OUT: ((0,), (1, 2)), GATE: ((0, 1), (2,)), EARLY: ((0, 1), (2,)), LATE: ((0, 1, 2),)}
LOCAL = {OUT: 0, GATE: 1024, EARLY: 2048, LATE: 2816}
BASE = {GATE: 0, EARLY: 2048, LATE: 3584}
WIDTH = {GATE: 1024, EARLY: 768, LATE: 512}
SPLIT = 12
eps = 1e-05
LOG2E = 1.4426950408889634
highest = lax.Precision.HIGHEST

TILES = (3584, 4096, 2048, 2560, 3072, 0, 512, 1024, 1536)
BACK_TILES = (0, 512, 1024, 1536, 2048, 2560, 3072, 3584, 4096)
PLAN = (
    (1, (("dn", 0),)),
    (2, (("own", GATE),)),
    (4, (("dn", 1),)),
    (6, (("one", OUT), ("dn", 2))),
    (8, (("dn", 3),)),
    (10, (("one", GATE),)),
    (12, (("two", OUT),)),
    (13, (("give", EARLY),)),
    (14, (("dn", 4),)),
    (15, (("own", EARLY), ("two", GATE))),
)


def place():
    dp, fsdp = lax.axis_index("dp"), lax.axis_index("fsdp")
    return {"x": (fsdp // 2) % 4, "y": (dp // 4) * 2 + fsdp // 8, "z": dp % 4, "c": fsdp % 2}


def device(at):
    y = at["y"]
    return ((y // 2) * 4 + at["z"], (y % 2) * 8 + at["x"] * 2 + at["c"])


def moved(at, axis, step):
    size = 2 if axis == "c" else 4
    return dict(at, **{axis: lax.rem(at[axis] + step, size)})


def greet(at):
    peers = [moved(at, axis, step) for axis in "xyz" for step in (1, 2, 3)] + [moved(at, "c", 1)]
    for peer in peers:
        pl.semaphore_signal(pltpu.get_barrier_semaphore(), inc=1, device_id=device(peer), device_id_type=MESH)


def meet():
    pl.semaphore_wait(pltpu.get_barrier_semaphore(), 10)


def remote(src, dst, send, recv, peer):
    return pltpu.make_async_remote_copy(
        src_ref=src, dst_ref=dst, send_sem=send, recv_sem=recv, device_id=device(peer), device_id_type=MESH
    )


def chips(at, full):
    every = slice(None)
    y, z, x = at["y"], at["z"], at["x"]
    return (
        every if "y" in full else y // 2,
        every if "z" in full else z,
        every if "y" in full else y % 2,
        every if "x" in full else x,
    )


def rolled_down(x, step):
    zeros = jnp.zeros((8, x.shape[1]), x.dtype)
    return pltpu.roll(jnp.concatenate([zeros, x], axis=0), step, axis=0)[8:]


def rolled_up(x, step):
    rows = x.shape[0]
    zeros = jnp.zeros((8, x.shape[1]), x.dtype)
    return pltpu.roll(jnp.concatenate([x, zeros], axis=0), rows + 8 - step, axis=0)[:rows]


def tile(j, base=0, size=128):
    return pl.ds(pl.multiple_of(base + j * size, 128), size)


def dot_nt(a, b):
    return lax.dot_general(a, b, (((1,), (1,)), ((), ())), preferred_element_type=jnp.float32)


def dot(a, b, **more):
    return jnp.dot(a, b, preferred_element_type=jnp.float32, **more)


def row_sum(x):
    return jnp.sum(x, axis=1, keepdims=True)


def col_sum(x):
    return jnp.sum(x, axis=0, keepdims=True)


def block_kernel(
    lengths,
    ids,
    in_shard_hbm,
    wo_hbm,
    tokens_hbm,
    cotangent_hbm,
    params_hbm,
    block_out_hbm,
    input_grad,
    gi_hbm,
    go_hbm,
    small_hbm,
    norm_hbm,
    full_in,
    in_shard,
    wo,
    tokens,
    cotangent,
    params,
    block_out,
    gi_out,
    go_out,
    small_out,
    norm_out,
    wi,
    other,
    blk,
    live,
    skip,
    full_out,
    work,
    proj,
    act,
    dsilu,
    y_ref,
    dinner,
    dproj,
    inner_t,
    normed,
    normed_t,
    mix,
    mix_t,
    cum_parts,
    key_parts,
    cum_t,
    key_t,
    step_ref,
    q_ref,
    m_ref,
    dcum_ref,
    dstep_ref,
    back_ref,
    taps,
    gain,
    norm_gain,
    part0,
    recv1,
    part1,
    recv2,
    part2,
    recv3,
    swap_from,
    swap_to,
    small_now,
    small_other,
    small_half,
    small_got,
    small_last,
    norm_now,
    norm_got,
    swap_sem,
    local_sem,
    edge_sem,
    ag_send,
    ag_recv,
    ag_pass,
    ag_got,
    rs_send,
    rs_recv,
    rs_pass,
    rs_got,
    small_send,
    small_recv,
    norm_send,
    norm_recv,
):
    low, full = jnp.bfloat16, jnp.float32
    at = place()
    core = at["c"]
    first = core == 0
    sibling = moved(at, "c", 1)
    here = chips(at, ())
    inputs = [
        pltpu.make_async_copy(source, target, edge_sem.at[i])
        for i, (source, target) in enumerate(
            (
                (in_shard_hbm, in_shard),
                (params_hbm, params),
                (tokens_hbm, tokens),
                (wo_hbm, wo),
                (cotangent_hbm, cotangent),
            )
        )
    ]
    for copy in inputs:
        copy.start()
    greet(at)

    lane = lax.broadcasted_iota(jnp.int32, (TOK, 128), 1)
    left = lane < HEAD
    row = lax.broadcasted_iota(jnp.int32, (TOK, TOK), 0)
    column = lax.broadcasted_iota(jnp.int32, (TOK, TOK), 1)
    for copy in inputs:
        copy.wait()
    wi[:, COLS - 256 :] = jnp.zeros((8, 256), full)
    wi[:, :PROJ] = in_shard[...].astype(full)
    wi[:, COLS - 128 :] = params[0:8, :]
    full_out[here + (core,)] = wo[...]
    length = lengths[ids[0]]
    live[...] = (lax.broadcasted_iota(jnp.int32, (TOK, 128), 0) < length).astype(full)
    m_ref[...] = jnp.zeros_like(m_ref)
    for j in range(D // 128):
        x = tokens[:, j * 128 : j * 128 + 128].astype(full)
        m_ref[...] += x * x
    token_scale = lax.rsqrt(row_sum(m_ref[...]) / D + eps)
    owner = lax.broadcasted_iota(jnp.int32, (128, INNER), 1) >> 6
    repeats = (lax.broadcasted_iota(jnp.int32, (128, INNER), 0) == owner).astype(full)
    skip[...] = dot(params[8:16, :], repeats, precision=highest)[2:3]
    heads = params[8:16, :]
    meet()

    swap = remote(wi, other, swap_sem.at[0], swap_sem.at[1], sibling)
    swap.start()

    def held(batch, part, reach):
        start, width = PARTS[batch][part]
        if batch == OUT:
            return full_out.at[chips(at, reach) + (core, slice(None), pl.ds(start, width))]
        spot = pl.multiple_of(core * WIDTH[batch] + start + BASE[batch], 128)
        return full_in.at[chips(at, reach) + (slice(None), pl.ds(spot, width))]

    flying = {}
    drained = []

    def hop(batch, part, phase):
        target = held(batch, part, ORDERS[part][:phase])
        source = target
        if phase == 0 and batch != OUT:
            start, width = PARTS[batch][part]
            source = blk.at[:, pl.ds(BASE[batch] // 2 + start, width)]
        flying[batch, part] = []
        for step in (1, 2, 3):
            slot = ((batch * 3 + part) * 3 + phase) * 3 + step - 1
            copy = remote(source, target, ag_send.at[slot], ag_recv.at[slot], moved(at, ORDERS[part][phase], step))
            copy.start()
            flying[batch, part].append(copy)
            drained.append(copy)

    def landed(batch, part):
        for copy in flying[batch, part]:
            copy.wait_recv()

    given = {}

    def give(batch):
        for part in range(3):
            landed(batch, part)
            region = held(batch, part, "xyz")
            slot = batch * 3 + part
            given[batch, part] = remote(region, region, ag_pass.at[slot], ag_got.at[slot], sibling)
            given[batch, part].start()
            drained.append(given[batch, part])

    def taken(batch):
        for part in range(3):
            given[batch, part].wait_recv()

    swap.wait()
    stores = []

    def begin(batch):
        base, width = BASE[batch], WIDTH[batch]
        lanes = pl.ds(pl.multiple_of(base + core * width, 128), width)
        mine, theirs = wi[:, lanes], other[:, lanes]
        blk[:, base // 2 : base // 2 + width] = jnp.concatenate(
            [jnp.where(first, mine, theirs), jnp.where(first, theirs, mine)], axis=0
        ).astype(low)
        launch(batch, 0)
        copy = pltpu.make_async_copy(
            blk.at[:, pl.ds(base // 2, width)], full_in.at[here + (slice(None), lanes)], local_sem.at[len(stores)]
        )
        copy.start()
        stores.append(copy)

    def launch(batch, phase):
        for part in range(3):
            if phase:
                landed(batch, part)
            hop(batch, part, phase)

    begin(LATE)
    begin(EARLY)
    begin(GATE)
    launch(OUT, 0)
    for copy in stores:
        copy.wait()
    launch(LATE, 1)
    launch(EARLY, 1)
    launch(LATE, 2)
    launch(GATE, 1)
    launch(EARLY, 2)
    launch(OUT, 1)

    def slot_of(slot):
        if slot < 2:
            return work.reshape(4, 4, 2, 4, 16, 512).at[pl.ds(2 * slot, 2)]
        return inner_t.reshape(2, 4, 2, 4, 2, 16, 512).at[:, :, :, :, slot - 2]

    def fetched(slot, start):
        source = full_in.at[:, :, :, :, :, pl.ds(start, 512)]
        return pltpu.make_async_copy(source, slot_of(slot), local_sem.at[3 + slot])

    def fetch(i):
        fetched(i % 4, TILES[i]).start()

    def weight(i):
        slot = i % 4
        fetched(slot, TILES[i]).wait()
        if slot < 2:
            return work[pl.ds(CHIPS * slot, CHIPS)].reshape(D, 512)
        return inner_t[:, slot - 2].reshape(D, 512)

    give(LATE)
    launch(GATE, 2)
    taken(LATE)
    fetch(1)
    fetch(0)
    give(EARLY)
    late = weight(1)
    packed = late[:, 384:]

    def spread(r, base, count, each):
        pick = (
            lax.broadcasted_iota(jnp.int32, (128, D), 0) * 8 + r == lax.broadcasted_iota(jnp.int32, (128, D), 1)
        ).astype(low)
        shared = dot(pick, packed).astype(low)
        line = lax.broadcasted_iota(jnp.int32, (128, count), 0).astype(full)
        spot = lax.broadcasted_iota(jnp.int32, (128, count), 1).astype(full) + base
        owner = jnp.floor((spot + 0.5) * (1.0 / each))
        found = dot(shared, (line == spot - owner * each).astype(low))
        return col_sum(jnp.where(line == owner, found, 0.0))

    norm_gain[...] = spread(0, 0, D, 8)
    for j in range(D // 128):
        cols = slice(j * 128, j * 128 + 128)
        value = (tokens[:, cols].astype(full) * token_scale * norm_gain[:, cols]).astype(low)
        normed[:, cols] = value
        normed_t[j * 8 : j * 8 + 8] = value.T.reshape(8, 16, TOK)

    def project(i, weights):
        width = weights.shape[1]
        proj[:, TILES[i] : TILES[i] + width] = dot(normed[...], weights)

    def convolve(begin, end):
        @pl.loop(begin, end)
        def _(j):
            cols = tile(j)
            x = proj[:, tile(j, INNER)]
            pre = taps[4:5, cols] + taps[3:4, cols] * x
            for step in (1, 2, 3):
                pre = pre + taps[3 - step : 4 - step, cols] * rolled_down(x, step)
            sig = jax.nn.sigmoid(pre)
            act[:, cols] = (pre * sig).astype(low)
            dsilu[:, cols] = (sig * (1.0 + pre * (1.0 - sig))).astype(low)

    project(1, late[:, :384])
    project(0, weight(0))
    taps[...] = jnp.zeros_like(taps)
    for base in (0, XBC // 2):
        for k in range(CONV + 1):
            taps[k : k + 1, base : base + XBC // 2] = spread((3, 4, 5, 6, 2)[k], base, XBC // 2, 18)
    gain[...] = spread(1, 0, INNER, 16)
    taken(EARLY)
    for i in (2, 3, 4):
        fetch(i)
    launch(OUT, 2)
    give(GATE)
    convolve(SPLIT, XBC // 128)

    raw = proj[:, INNER + XBC : INNER + XBC + 128] + heads[0:1, :]
    grown = jnp.exp(-jnp.abs(raw))
    more = 1.0 + grown
    logged = jnp.where(more == 1.0, grown, jnp.log(more) * grown / jnp.where(more == 1.0, 1.0, more - 1.0))
    steps = jnp.where(lane < HEADS, jnp.maximum(raw, 0.0) + logged, 0.0)
    rate = -jnp.exp(heads[1:2, :])

    def split(x):
        top = x.astype(low)
        middle = (x - top.astype(full)).astype(low)
        return top, middle, (x - top.astype(full) - middle.astype(full)).astype(low)

    def summed(mask, x):
        found = dot(jnp.where(mask, 1.0, 0.0).astype(low), jnp.concatenate(split(x), axis=1))
        return found[:, :128] + found[:, 128:256] + found[:, 256:]

    cum = summed(row >= column, steps * rate) * LOG2E
    step_ref[...] = steps
    key = cum - jnp.log2(jnp.maximum(steps, 1e-37))
    turned, key_turned = cum.T, key.T
    for head in range(HEADS):
        cum_t[head] = turned[head : head + 1]
        key_t[head] = key_turned[head : head + 1]

    def thirds(x):
        top, middle, rest = [part.astype(full) for part in split(jnp.where(lane < HEADS, x, 0.0))]
        return (top + pltpu.roll(middle, HEADS, axis=1) + pltpu.roll(rest, 2 * HEADS, axis=1)).astype(low)

    cum_parts[...] = thirds(cum)
    key_parts[...] = thirds(key)
    mixed = jnp.where(row >= column, dot_nt(act[:, INNER + STATE :], act[:, INNER : INNER + STATE]), 0.0)
    mix[...] = mixed
    mix_t[...] = mixed.T

    for i in (2, 3, 4):
        project(i, weight(i))
    taken(GATE)
    for i in (5, 6, 7, 8):
        fetch(i)
    convolve(0, SPLIT)
    for i in (5, 6, 7, 8):
        project(i, weight(i))
    give(OUT)
    q_ref[...] = jnp.zeros_like(q_ref)
    dcum_ref[...] = jnp.zeros_like(dcum_ref)
    dstep_ref[...] = jnp.zeros_like(dstep_ref)

    causal = lax.broadcasted_iota(jnp.int32, (128, 128), 0) >= lax.broadcasted_iota(jnp.int32, (128, 128), 1)

    anti = lax.broadcasted_iota(jnp.int32, (128, 128), 0) <= lax.broadcasted_iota(jnp.int32, (128, 128), 1)

    def spread_heads(parts, j):
        line = lax.broadcasted_iota(jnp.int32, (128, 256), 0)
        head = 2 * j + (lax.broadcasted_iota(jnp.int32, (128, 256), 1) >> 7)
        return dot(parts[...], jnp.where(((line & 31) == head) & (line < 96), 1.0, 0.0).astype(low))

    @pl.loop(0, HEADS // 2)
    def _(j):
        cols = tile(j)
        cums = spread_heads(cum_parts, j)
        values = act[:, cols]
        for block in range(TOK // 128):
            start, last = block * 128, block * 128 + 128
            halves = []
            for e in (0, 1):
                pieces = []
                for past in range(block + 1):
                    span = slice(past * 128, past * 128 + 128)
                    gap = cums[start:last, e * 128 : e * 128 + 128] - key_t[2 * j + e, :, span]
                    if past == block:
                        gap = jnp.where(causal, gap, -1e30)
                    pieces.append((mix[start:last, span] * jnp.exp2(gap)).astype(low))
                halves.append(jnp.concatenate(pieces, axis=1))
            found = dot(jnp.concatenate(halves, axis=0), values[:last])
            y = jnp.where(left[:128], found[:128], found[128:]) + skip[:, cols] * values[start:last].astype(full)
            y_ref[start:last, cols] = y
            gate = proj[start:last, cols]
            gated = y * gate * jax.nn.sigmoid(gate)
            q_ref[start:last] += gated * gated

    q_ref[...] = jnp.broadcast_to(lax.rsqrt(row_sum(q_ref[...]) / INNER + eps), (TOK, 128))
    mix[...] = jnp.zeros_like(mix)

    @pl.loop(0, INNER // 128)
    def _(j):
        cols = tile(j)
        gate = proj[:, cols]
        gated = y_ref[:, cols] * gate * jax.nn.sigmoid(gate)
        value = (gated * q_ref[...] * gain[:, cols]).astype(low)
        dproj[:, cols] = value
        inner_t[pl.ds(4 * j, 4)] = value.T.reshape(4, 2, 16, TOK)

    for j in range(D // 128):
        cols = slice(j * 128, j * 128 + 128)
        normed[:, cols] = (live[...] * cotangent[:, cols].astype(full)).astype(low)

    def grads(batch, group, side, half):
        start = PARTS[batch][group[0]][0]
        width = sum(PARTS[batch][part][1] for part in group)
        if batch == OUT:
            lhs = inner_t[pl.ds(32 * half, 32), side].reshape(TOK, TOK)
            rhs = normed[:, start : start + width]
        else:
            lhs = normed_t[pl.ds(32 * half, 32)].reshape(TOK, TOK)
            rhs = dproj[:, pl.ds(pl.multiple_of(BASE[batch] + start + side * WIDTH[batch], 128), width)]
        value = dot(lhs, rhs)
        return [(part, PARTS[batch][part][0] - start, PARTS[batch][part][1], value) for part in group]

    def spot_of(part, half, m):
        spot = {"y": 2 * half + (m // 4) % 2, "z": m // 8, "x": m % 4}
        axes = ORDERS[part]
        return spot[axes[2]] * 16 + spot[axes[1]] * 4 + spot[axes[0]]

    users = [[], []]

    def rs_free():
        for gone in users:
            while gone:
                rs_pass_copy(*gone.pop()).wait_send()

    def rs_give(batch):
        for slot, group in enumerate(GROUPS[batch]):
            while users[slot]:
                rs_pass_copy(*users[slot].pop()).wait_send()
            for half in (0, 1):
                for part, offset, width, value in grads(batch, group, 1 - core, half):
                    value = value[:, offset : offset + width].astype(low)
                    for m in range(32):
                        work[CHIPS * slot + spot_of(part, half, m), :, offset : offset + width] = value[
                            16 * m : 16 * m + 16
                        ]
            for part in group:
                offset = PARTS[batch][part][0] - PARTS[batch][group[0]][0]
                users[slot].append((batch, part, slot, offset))
                rs_pass_copy(batch, part, slot, offset).start()

    def rs_pass_copy(batch, part, slot=0, offset=0):
        width = PARTS[batch][part][1]
        sem = batch * 3 + part
        return remote(
            work.at[pl.ds(CHIPS * slot, CHIPS), :, pl.ds(offset, width)],
            part0.at[:, :, lanes_of(batch, part)],
            rs_pass.at[sem],
            rs_got.at[sem],
            sibling,
        )

    def lanes_of(batch, part):
        start, width = PARTS[batch][part]
        return pl.ds(LOCAL[batch] + start, width)

    def rs_copies(batch, part, stage):
        lanes = lanes_of(batch, part)
        axis = ORDERS[part][3 - stage]
        copies = []
        for step in (1, 2, 3):
            peer = moved(at, axis, step)
            there, slot = peer[axis], pl.ds(step - 1, 1)
            if stage == 1:
                source, target = part0.at[pl.ds(there * 16, 16), :, lanes], recv1.at[pl.ds(16 * step - 16, 16), :, lanes]
            elif stage == 2:
                source, target = part1.at[pl.ds(there * 4, 4), :, lanes], recv2.at[pl.ds(4 * step - 4, 4), :, lanes]
            else:
                source, target = part2.at[pl.ds(there, 1), :, lanes], recv3.at[slot, :, lanes]
            sem = ((batch * 3 + part) * 3 + stage - 1) * 3 + step - 1
            copies.append(remote(source, target, rs_send.at[sem], rs_recv.at[sem], peer))
        return copies

    def rs_hop(batch, part, stage):
        for copy in rs_copies(batch, part, stage):
            copy.start()

    def rs_landed(batch, part, stage):
        for copy in rs_copies(batch, part, stage):
            copy.wait_recv()

    def rs_own(batch):
        for group in GROUPS[batch]:
            for part in group:
                rs_pass_copy(batch, part).wait_recv()
            for half in (0, 1):
                for part, offset, width, value in grads(batch, group, core, half):
                    lanes = lanes_of(batch, part)
                    for m in range(32):
                        now = pl.ds(spot_of(part, half, m), 1)
                        piece = value[16 * m : 16 * m + 16, offset : offset + width][None]
                        part0[now, :, lanes] = (piece + part0[now, :, lanes].astype(full)).astype(low)
            for part in group:
                rs_hop(batch, part, 1)

    def rs_one(batch, part):
        lanes = lanes_of(batch, part)
        rs_landed(batch, part, 1)
        mine = at[ORDERS[part][2]] * 16
        for i in range(16):
            now = pl.ds(i, 1)
            value = part0[pl.ds(mine + i, 1), :, lanes].astype(full)
            for k in range(3):
                value = value + recv1[pl.ds(16 * k + i, 1), :, lanes].astype(full)
            part1[now, :, lanes] = value.astype(low)
        rs_hop(batch, part, 2)

    def rs_two(batch, part):
        lanes = lanes_of(batch, part)
        rs_landed(batch, part, 2)
        mine = at[ORDERS[part][1]] * 4
        for i in range(4):
            now = pl.ds(i, 1)
            value = part1[pl.ds(mine + i, 1), :, lanes].astype(full)
            for k in range(3):
                value = value + recv2[pl.ds(4 * k + i, 1), :, lanes].astype(full)
            part2[now, :, lanes] = value.astype(low)
        rs_hop(batch, part, 3)

    def rs_three(batch, part):
        lanes = lanes_of(batch, part)
        rs_landed(batch, part, 3)
        value = part2[pl.ds(at[ORDERS[part][0]], 1), :, lanes].astype(full)
        for k in range(3):
            value = value + recv3[pl.ds(k, 1), :, lanes].astype(full)
        value = value[0]
        start, width = PARTS[batch][part]
        if batch == OUT:
            go_out[:, start : start + width] = value
            return
        base = BASE[batch]
        at_column = pl.multiple_of(base + core * WIDTH[batch] + start, 128)
        gi_out[:, pl.ds(at_column, width)] = jnp.where(first, value[:8], value[8:])
        swap_from[:, pl.ds(base // 2 + start, width)] = jnp.where(first, value[8:], value[:8])

    rs_give(OUT)
    taken(OUT)
    while drained:
        drained.pop().wait_send()
    wout = full_out.reshape(INNER, D)
    wide_live = jnp.concatenate([live[...], live[...]], axis=1)

    m_ref[...] = jnp.zeros_like(m_ref)

    @pl.loop(0, D // 256)
    def _(j):
        cols = tile(j, 0, 256)
        branch = dot(dproj[:, :INNER], wout[:, cols])
        block_out[:, cols] = (tokens[:, cols].astype(full) + wide_live * branch).astype(low)
        shares = normed[:, cols].astype(full) * branch
        m_ref[...] += shares[:, :128] + shares[:, 128:]

    outputs = [pltpu.make_async_copy(block_out, block_out_hbm, edge_sem.at[5])]
    outputs[0].start()

    m_ref[...] = jnp.broadcast_to(row_sum(m_ref[...]) / INNER, (TOK, 128))

    @pl.loop(0, INNER // 256)
    def _(j):
        wide = tile(j, 0, 256)
        sums = [jnp.zeros((1, 128), full)] * 2
        for rows in (slice(0, 256), slice(256, 512)):
            value = dot_nt(normed[rows, :], wout[wide, :])
            for half in (0, 1):
                cols = tile(2 * j + half)
                inside = value[:, half * 128 : half * 128 + 128]
                y, gate, q = y_ref[rows, cols], proj[rows, cols], q_ref[rows, :]
                sig = jax.nn.sigmoid(gate)
                silu = gate * sig
                u = y * silu * q
                sums[half] = sums[half] + col_sum(inside * u)
                dgated = q * (inside * gain[:, cols] - u * m_ref[rows, :])
                dproj[rows, cols] = (dgated * y * (sig + silu * (1.0 - sig))).astype(low)
                dinner[rows, cols] = dgated * silu
        for half in (0, 1):
            small_now[5:6, tile(2 * j + half)] = sums[half]

    rs_own(OUT)

    rs_give(GATE)

    dnormed = proj.at[:, pl.ds(0, D)]

    def back_load(i):
        fetched(2 + i % 2, BACK_TILES[i]).start()

    def back_tile(i):
        start = BACK_TILES[i]
        fetched(2 + i % 2, start).wait()
        value = dot_nt(dproj[:, start : start + 512], inner_t[:, i % 2].reshape(D, 512))
        dnormed[...] = value if i == 0 else dnormed[...] + value
        if i + 2 < len(BACK_TILES):
            back_load(i + 2)

    back_load(0)
    back_load(1)

    def conv_back(dact, j):
        cols = tile(j)
        x = proj[:, tile(j, INNER)]
        dpre = dact * dsilu[:, cols].astype(full)
        small_now[4:5, cols] = col_sum(dpre)
        small_now[3:4, cols] = col_sum(dpre * x)
        dx = taps[3:4, cols] * dpre
        for step in (1, 2, 3):
            moved_up = rolled_up(dpre, step)
            small_now[3 - step : 4 - step, cols] = col_sum(moved_up * x)
            dx = dx + taps[3 - step : 4 - step, cols] * moved_up
        dproj[:, tile(j, INNER)] = dx.astype(low)

    back_ref[...] = jnp.zeros_like(back_ref)

    def settle(j):
        cols = tile(j)
        values, dy, back = act[:, cols].astype(full), dinner[:, cols], back_ref[...]
        direct = values * back
        crossing = dy.astype(low).astype(full) * (y_ref[:, cols] - skip[:, cols] * values) - direct
        small_now[7:8, cols] = col_sum(dy * values)
        for e in (0, 1):
            mine = left if e == 0 else jnp.logical_not(left)
            spot = lane == 2 * j + e
            dcum_ref[...] = jnp.where(spot, row_sum(jnp.where(mine, crossing, 0.0)), dcum_ref[...])
            dstep_ref[...] = jnp.where(spot, row_sum(jnp.where(mine, direct, 0.0)), dstep_ref[...])
        conv_back(back + skip[:, cols] * dy, j)

    @pl.loop(0, HEADS // 2)
    def _(j):
        for turn, events in PLAN:

            @pl.when(j == turn)
            def _(events=events):
                for action, what in events:
                    if action == "dn":
                        back_tile(what)
                    elif action in ("give", "own"):
                        {"give": rs_give, "own": rs_own}[action](what)
                    else:
                        for part in range(3):
                            {"one": rs_one, "two": rs_two, "three": rs_three}[action](what, part)

        settle(jnp.maximum(j - 1, 0))
        cols = tile(j)
        keys = spread_heads(key_parts, j)
        v_low = act[:, cols]
        dy_low = dinner[:, cols].astype(low)
        own = (jnp.where(left, v_low, jnp.zeros_like(v_low)), jnp.where(left, jnp.zeros_like(v_low), v_low))
        found = []
        for block in range(TOK // 128):
            start, last = block * 128, block * 128 + 128
            both = dot_nt(jnp.concatenate([own[0][start:last], own[1][start:last]], axis=0), dy_low[start:])
            halves = []
            total = None
            for e in (0, 1):
                pieces, shares = [], []
                for later in range(block, TOK // 128):
                    span = slice(later * 128, later * 128 + 128)
                    gap = cum_t[2 * j + e, :, span] - keys[start:last, e * 128 : e * 128 + 128]
                    if later == block:
                        gap = jnp.where(anti, gap, -1e30)
                    decay = jnp.exp2(gap)
                    pieces.append((mix_t[start:last, span] * decay).astype(low))
                    inside = slice((later - block) * 128, (later - block + 1) * 128)
                    shares.append(both[e * 128 : e * 128 + 128, inside] * decay)
                halves.append(jnp.concatenate(pieces, axis=1))
                share = jnp.concatenate(shares, axis=1)
                total = share if total is None else total + share
            mix[start:last, start:] += total
            given_back = dot(jnp.concatenate(halves, axis=0), dy_low[start:])
            found.append(jnp.where(left[:128], given_back[:128], given_back[128:]))
        for block, value in enumerate(found):
            back_ref[block * 128 : block * 128 + 128] = value

    settle(HEADS // 2 - 1)
    masked = jnp.where(row <= column, mix[...], 0.0)
    conv_back(dot(masked.astype(low), act[:, INNER + STATE :]), INNER // 128)
    conv_back(dot(masked.T.astype(low), act[:, INNER : INNER + STATE]), INNER // 128 + 1)
    dacc = summed(row <= column, dcum_ref[...])
    sig = jax.nn.sigmoid(proj[:, INNER + XBC : INNER + XBC + 128] + heads[0:1, :])
    steps = step_ref[...]
    ratio = jnp.where(steps > 1e-30, sig / jnp.maximum(steps, 1e-30), 1.0)
    draw = jnp.where(lane < HEADS, dstep_ref[...] * ratio + dacc * rate * sig, 0.0)
    dproj[:, INNER + XBC : INNER + XBC + 128] = draw.astype(low)
    dproj[:, INNER + XBC + 128 :] = jnp.zeros((TOK, 128), low)
    small_now[6:7, :] = jnp.zeros((1, XBC), full)
    small_now[6:7, :128] = col_sum(draw)
    small_now[6:7, 128:256] = rate * col_sum(dacc * steps)
    small_now[5:6, INNER:] = jnp.zeros((1, XBC - INNER), full)
    small_now[7:8, INNER:] = jnp.zeros((1, XBC - INNER), full)


    def small_swap():
        away = pl.ds(pl.multiple_of((1 - core) * HALF, 128), HALF)
        return remote(small_now.at[:, away], small_other, small_send.at[0], small_recv.at[0], sibling)

    def small_copies(stage):
        made = []
        for part in range(3):
            lanes = pl.ds(part * THIRD, THIRD)
            axis = ORDERS[part][stage - 1]
            for step in (1, 2, 3):
                slot = (stage - 1) * 3 + step - 1
                sem = slot * 3 + part + 1
                made.append(
                    remote(
                        small_half.at[stage - 1, :, lanes],
                        small_got.at[slot, :, lanes],
                        small_send.at[sem],
                        small_recv.at[sem],
                        moved(at, axis, step),
                    )
                )
        return made

    def small_back():
        return remote(small_half.at[3], small_last, small_send.at[28], small_recv.at[28], sibling)

    def small_add(stage):
        if stage == 0:
            small_swap().wait_recv()
            mine = pl.ds(pl.multiple_of(core * HALF, 128), HALF)
            small_half[0] = small_now[:, mine] + small_other[...]
        else:
            for copy in small_copies(stage):
                copy.wait_recv()
            value = small_half[stage - 1]
            for k in range(3):
                value = value + small_got[(stage - 1) * 3 + k]
            small_half[stage] = value
        for copy in small_copies(stage + 1) if stage < 3 else [small_back()]:
            copy.start()
            drained.append(copy)

    def norm_copies(stage):
        made = []
        for step in (1,) if stage == 0 else (1, 2, 3):
            slot = 0 if stage == 0 else stage * 3 - 3 + step
            peer = moved(at, "cxyz"[stage], step)
            made.append(remote(norm_now.at[stage], norm_got.at[slot], norm_send.at[slot], norm_recv.at[slot], peer))
        return made

    def norm_start(stage):
        for copy in norm_copies(stage):
            copy.start()
            drained.append(copy)

    def norm_add(stage):
        value = norm_now[stage]
        for k, copy in enumerate(norm_copies(stage)):
            copy.wait_recv()
            value = value + norm_got[0 if stage == 0 else stage * 3 - 2 + k]
        if stage == 3:
            norm_out[...] = value
        else:
            norm_now[stage + 1] = value
            norm_start(stage + 1)

    def drain():
        while drained:
            drained.pop().wait_send()

    small_swap().start()
    drained.append(small_swap())
    rs_give(LATE)
    back_tile(5)
    small_add(0)
    back_tile(6)
    rs_own(LATE)
    back_tile(7)
    small_add(1)
    back_tile(8)
    m_ref[...] = jnp.zeros_like(m_ref)
    for j in range(D // 128):
        cols = slice(j * 128, j * 128 + 128)
        u = tokens[:, cols].astype(full) * token_scale
        du = dnormed[:, cols] * u
        norm_now[0, j : j + 1, :] = col_sum(du)
        m_ref[...] += du * norm_gain[:, cols]
    mean = row_sum(m_ref[...]) / D
    norm_start(0)
    for part in range(3):
        rs_one(EARLY, part)
    for j in range(D // 128):
        cols = slice(j * 128, j * 128 + 128)
        u = tokens[:, cols].astype(full) * token_scale
        du = dnormed[:, cols] * norm_gain[:, cols]
        normed[:, cols] = (cotangent[:, cols].astype(full) + token_scale * (du - u * mean)).astype(low)
    final = pltpu.make_async_copy(normed, input_grad, local_sem.at[0])
    final.start()
    norm_add(0)
    for part in range(3):
        rs_three(OUT, part)
    for part in range(3):
        rs_three(GATE, part)
    for batch in (OUT, GATE):
        for part in range(3):
            for stage in (1, 2, 3):
                for copy in rs_copies(batch, part, stage):
                    copy.wait_send()
    small_add(2)
    norm_add(1)
    for part in range(3):
        rs_one(LATE, part)
    for part in range(3):
        rs_two(EARLY, part)
    small_add(3)
    norm_add(2)
    for part in range(3):
        rs_two(LATE, part)
    for part in range(3):
        rs_three(EARLY, part)
    small_back().wait_recv()
    mine = pl.ds(pl.multiple_of(core * HALF, 128), HALF)
    small_out[:, mine] = small_half[3]
    small_out[:, pl.ds(pl.multiple_of((1 - core) * HALF, 128), HALF)] = small_last[...]
    outputs.append(pltpu.make_async_copy(small_out, small_hbm, edge_sem.at[6]))
    outputs.append(pltpu.make_async_copy(go_out, go_hbm, edge_sem.at[7]))
    for copy in outputs[1:]:
        copy.start()
    rs_free()
    norm_add(3)
    outputs.append(pltpu.make_async_copy(norm_out, norm_hbm, edge_sem.at[8]))
    outputs[3].start()
    drain()
    for part in range(3):
        rs_three(LATE, part)
    last = remote(swap_from, swap_to, swap_sem.at[2], swap_sem.at[3], sibling)
    last.start()
    for batch in (EARLY, LATE):
        for part in range(3):
            for stage in (1, 2, 3):
                for copy in rs_copies(batch, part, stage):
                    copy.wait_send()
    final.wait()
    last.wait()
    for batch in (GATE, EARLY, LATE):
        base, width = BASE[batch], WIDTH[batch]
        lanes = pl.ds(pl.multiple_of(base + (1 - core) * width, 128), width)
        gi_out[:, lanes] = swap_to[:, base // 2 : base // 2 + width]
    outputs.append(pltpu.make_async_copy(gi_out, gi_hbm, edge_sem.at[9]))
    outputs[4].start()
    for copy in outputs:
        copy.wait()


def block(lengths, ids, in_shard, wo, tokens, cotangent, params):
    full, low = jnp.float32, jnp.bfloat16
    anywhere = pl.BlockSpec(memory_space=pl.ANY)
    sems = pltpu.SemaphoreType.DMA
    return pl.pallas_call(
        block_kernel,
        out_shape=(
            jax.ShapeDtypeStruct((TOK, D), low),
            jax.ShapeDtypeStruct((TOK, D), low),
            jax.ShapeDtypeStruct((8, COLS), full),
            jax.ShapeDtypeStruct((16, D), full),
            jax.ShapeDtypeStruct((8, XBC), full),
            jax.ShapeDtypeStruct((8, 128), full),
            jax.ShapeDtypeStruct((2, 4, 2, 4, 16, COLS), low),
        ),
        in_specs=[pl.BlockSpec(memory_space=pltpu.SMEM)] * 2 + [anywhere] * 5,
        out_specs=[anywhere] * 7,
        scratch_shapes=[
            pltpu.VMEM((8, PROJ), low),
            pltpu.VMEM((16, D), low),
            pltpu.VMEM((TOK, D), low),
            pltpu.VMEM((TOK, D), low),
            pltpu.VMEM((16, 128), full),
            pltpu.VMEM((TOK, D), low),
            pltpu.VMEM((8, COLS), full),
            pltpu.VMEM((16, D), full),
            pltpu.VMEM((8, XBC), full),
            pltpu.VMEM((8, 128), full),
            pltpu.VMEM((8, COLS), full),
            pltpu.VMEM((8, COLS), full),
            pltpu.VMEM((16, XBC), low),
            pltpu.VMEM((TOK, 128), full),
            pltpu.VMEM((1, INNER), full),
            pltpu.VMEM((2, 4, 2, 4, 2, 16, D), low),
            pltpu.VMEM((2 * CHIPS, 16, 512), low),
            pltpu.VMEM((TOK, COLS - 128), full),
            pltpu.VMEM((TOK, XBC), low),
            pltpu.VMEM((TOK, XBC), low),
            pltpu.VMEM((TOK, INNER), full),
            pltpu.VMEM((TOK, INNER), full),
            pltpu.VMEM((TOK, COLS), low),
            pltpu.VMEM((CHIPS, 2, 16, TOK), low),
            pltpu.VMEM((TOK, D), low),
            pltpu.VMEM((CHIPS, 16, TOK), low),
            pltpu.VMEM((TOK, TOK), full),
            pltpu.VMEM((TOK, TOK), full),
            pltpu.VMEM((TOK, 128), low),
            pltpu.VMEM((TOK, 128), low),
            pltpu.VMEM((HEADS, 1, TOK), full),
            pltpu.VMEM((HEADS, 1, TOK), full),
            pltpu.VMEM((TOK, 128), full),
            pltpu.VMEM((TOK, 128), full),
            pltpu.VMEM((TOK, 128), full),
            pltpu.VMEM((TOK, 128), full),
            pltpu.VMEM((TOK, 128), full),
            pltpu.VMEM((TOK, 128), full),
            pltpu.VMEM((8, XBC), full),
            pltpu.VMEM((1, INNER), full),
            pltpu.VMEM((1, D), full),
            pltpu.VMEM((CHIPS, 16, SIDE), low),
            pltpu.VMEM((48, 16, SIDE), low),
            pltpu.VMEM((16, 16, SIDE), low),
            pltpu.VMEM((12, 16, SIDE), low),
            pltpu.VMEM((4, 16, SIDE), low),
            pltpu.VMEM((3, 16, SIDE), low),
            pltpu.VMEM((8, XBC), full),
            pltpu.VMEM((8, XBC), full),
            pltpu.VMEM((8, XBC), full),
            pltpu.VMEM((8, HALF), full),
            pltpu.VMEM((4, 8, HALF), full),
            pltpu.VMEM((9, 8, HALF), full),
            pltpu.VMEM((8, HALF), full),
            pltpu.VMEM((4, 8, 128), full),
            pltpu.VMEM((10, 8, 128), full),
            sems((4,)),
            sems((7,)),
            sems((10,)),
            sems((108,)),
            sems((108,)),
            sems((12,)),
            sems((12,)),
            sems((108,)),
            sems((108,)),
            sems((12,)),
            sems((12,)),
            sems((29,)),
            sems((29,)),
            sems((10,)),
            sems((10,)),
        ],
        compiler_params=pltpu.CompilerParams(collective_id=0, has_side_effects=True, vmem_limit_bytes=63 << 20),
    )(lengths, ids, in_shard, wo, tokens, cotangent, params)


def finish_kernel(
    out_in,
    grad_in,
    gi_in,
    go_in,
    small_in,
    norm_in,
    out_hbm,
    grad_hbm,
    gain_hbm,
    gi_hbm,
    conv_hbm,
    bias_hbm,
    dt_hbm,
    log_hbm,
    skip_hbm,
    inner_hbm,
    go_hbm,
    small,
    norm,
    gi,
    go,
    out,
    grad,
    gain_out,
    gi_out,
    conv_out,
    bias_out,
    dt_out,
    log_out,
    skip_out,
    inner_out,
    sem,
):
    pairs = ((small_in, small), (norm_in, norm), (gi_in, gi), (go_in, go), (out_in, out), (grad_in, grad))
    copies = [pltpu.make_async_copy(source, target, sem.at[i]) for i, (source, target) in enumerate(pairs)]
    for copy in copies:
        copy.start()
    writes = []

    def write(source, target):
        writes.append(pltpu.make_async_copy(source, target, sem.at[len(copies) + len(writes)]))
        writes[-1].start()

    me = lax.axis_index("dp") * 16 + lax.axis_index("fsdp")
    copies[0].wait()

    def from_lane(count):
        return pltpu.roll(small[...], lax.rem(XBC - count * me, XBC), axis=1)

    conv = from_lane(18)
    conv_out[...] = conv[:CONV, :18]
    write(conv_out, conv_hbm)
    bias_out[...] = conv[CONV : CONV + 1, :18]
    write(bias_out, bias_hbm)
    inner_out[...] = from_lane(16)[5:6, :16]
    write(inner_out, inner_hbm)
    dt_out[...] = small[6:7, :HEADS]
    write(dt_out, dt_hbm)
    log_out[...] = small[6:7, 128 : 128 + HEADS]
    write(log_out, log_hbm)
    copies[4].wait()
    write(out, out_hbm)
    copies[5].wait()
    write(grad, grad_hbm)
    copies[2].wait()
    gi_out[...] = gi[:, :PROJ]
    write(gi_out, gi_hbm)
    copies[3].wait()
    write(go, go_hbm)
    owner = lax.broadcasted_iota(jnp.int32, (INNER, 128), 0) >> 6
    sums = (owner == lax.broadcasted_iota(jnp.int32, (INNER, 128), 1)).astype(jnp.float32)
    skip_out[...] = dot(small[:, :INNER], sums, precision=highest)[7:8, :HEADS]
    write(skip_out, skip_hbm)
    copies[1].wait()
    line = lax.broadcasted_iota(jnp.int32, (8, 128), 0)
    row = jnp.sum(jnp.where(line == me // 16, norm[...], 0.0), axis=0, keepdims=True)
    gain_out[...] = pltpu.roll(row, lax.rem(128 - 8 * lax.rem(me, 16), 128), axis=1)[:, :8]
    write(gain_out, gain_hbm)
    for copy in writes:
        copy.wait()


def finish(out, grad, gi, go, small, norm):
    full = jnp.float32
    anywhere = pl.BlockSpec(memory_space=pl.ANY)
    rest = [(CONV, 18), (1, 18), (1, HEADS), (1, HEADS), (1, HEADS), (1, 16)]
    shapes = [(1, 8), (8, PROJ)] + rest
    return pl.pallas_call(
        finish_kernel,
        out_shape=[jax.ShapeDtypeStruct(out.shape, out.dtype)] * 2
        + [jax.ShapeDtypeStruct(shape, full) for shape in shapes + [(16, D)]],
        in_specs=[anywhere] * 6,
        out_specs=[anywhere] * 11,
        scratch_shapes=[
            pltpu.VMEM(small.shape, full),
            pltpu.VMEM(norm.shape, full),
            pltpu.VMEM(gi.shape, full),
            pltpu.VMEM(go.shape, full),
            pltpu.VMEM(out.shape, out.dtype),
            pltpu.VMEM(out.shape, out.dtype),
        ]
        + [pltpu.VMEM(shape, full) for shape in shapes]
        + [pltpu.SemaphoreType.DMA((17,))],
        compiler_params=pltpu.CompilerParams(vmem_limit_bytes=62 << 20),
    )(out, grad, gi, go, small, norm)


def body(
    tokens,
    lengths,
    placement_ids,
    norm_gain,
    in_weight,
    conv_weight,
    conv_bias,
    dt_bias,
    a_log,
    d_skip,
    inner_gain,
    out_weight,
    cotangent,
):
    full = jnp.float32

    def line(values, first):
        values = values.astype(full).reshape(-1, values.shape[-1])
        rows, lanes = values.shape
        return jnp.pad(values, ((first, 16 - first - rows), (0, 128 - lanes)))

    params = (
        line(norm_gain, 0)
        + line(inner_gain, 1)
        + line(conv_bias, 2)
        + line(conv_weight, 3)
        + line(dt_bias, 8)
        + line(a_log, 9)
        + line(d_skip, 10)
    )
    block_out, input_grad, shard_in, shard_out, small, norm, _ = block(
        lengths, placement_ids, in_weight, out_weight, tokens, cotangent, params
    )
    found = finish(block_out, input_grad, shard_in, shard_out, small, norm)
    flat = [0, 0, 1, 0, 0, 1, 1, 1, 1, 1, 0]
    return tuple(value[0] if one else value for value, one in zip(found, flat))


def solution(mesh):
    placed = (
        P(("dp", "fsdp"), None),
        P(),
        P(("dp", "fsdp")),
        P(("dp", "fsdp")),
        P(("dp", "fsdp"), None),
        P(None, ("dp", "fsdp")),
        P(("dp", "fsdp")),
        P(),
        P(),
        P(),
        P(("dp", "fsdp")),
        P(("dp", "fsdp"), None),
        P(("dp", "fsdp"), None),
    )
    return jax.shard_map(
        body,
        mesh=mesh,
        in_specs=placed,
        out_specs=(
            P(("dp", "fsdp"), None),
            P(("dp", "fsdp"), None),
            P(("dp", "fsdp")),
            P(("dp", "fsdp"), None),
            P(None, ("dp", "fsdp")),
            P(("dp", "fsdp")),
            P(),
            P(),
            P(),
            P(("dp", "fsdp")),
            P(("dp", "fsdp"), None),
        ),
        check_vma=False,
    )
```

time: 195 us -> 149 us (0.76)
  local copies, waits for them, and re-layouts: 20.2 us -> 0 us
  Pallas kernels: 166 us -> 146 us
  other arithmetic: 4.52 us -> 1.36 us
    pallas_call x1, Pallas kernels: 166 us -> 142 us  [block(): pl.pallas_call(block_kernel, out_shape=(jax.ShapeDtypeStruct((TOK, D), lo...]
    unnamed x3 -> x0, local copies, waits for them, and re-layouts: 6 us -> none
    squeeze x4 -> x0, local copies, waits for them, and re-layouts: 4.25 us -> none  [the longest x1 1.27 us: body(): lax.dynamic_slice(small, (6, me * 8), (1, 8))[0]]
    concatenate x2 -> x0, local copies, waits for them, and re-layouts: 3.06 us -> none  [the longest x1 2.09 us: body(): jnp.concatenate([norm_gain, inner_gain, conv_bias, conv_weight.reshape(-1...]
    pallas_call x0 -> x1, Pallas kernels: none -> 3.03 us  [finish(): pl.pallas_call(finish_kernel, out_shape=[jax.ShapeDtypeStruct(out.shape,...]
    slice x3 -> x0, local copies, waits for them, and re-layouts: 3.02 us -> none  [the longest x1 1.58 us: body(): shard_in[:, :PROJ]]
where the time goes in v2:
time: 149 us; the launch traced here: 148 us
  Pallas kernels  146 us (98%)
  between operations  1.5 us (1%)
    pallas_call x1, Pallas kernels, block(): pl.pallas_call(block_kernel, out_shape=(jax.ShapeDtypeStruct((TOK, D), lo...  142 us
    pallas_call x1, Pallas kernels, finish(): pl.pallas_call(finish_kernel, out_shape=[jax.ShapeDtypeStruct(out.shape,...  3.03 us

profile of v2, /device:TPU:1, one launch (start us, length us, event | category | flops | bytes accessed | tf_op | source)
XLA Modules:
  0.0 148.4 jit_solution(16661137328656459644)
XLA Ops:
  1.3 1.4 pad_add_fusion.params_hbm
  2.7 142.5 %shard_map.212 = (bf16[512,1024]{1,0:T(8,128)(2,1)}, bf16[512,1024]{1,0:T(8,128)(2,1)}, f32[8,4608]{1,0:T(8,128)}, f32[16,1024]{1,0:T(8,128)}, f32[8,2304]{1,0:T...) custom-call(s32[128]{0:T(128)} %lengths.1, s32[1]{0:T(128)S(6)} %copy.24.ids, ...), custom_call_target="tpu_custom_call" | custom-call | tf_op jit(solution)/shard_map/pallas_call | solution.py:963
  145.1 3.0 %shard_map.213 = (bf16[512,1024]{1,0:T(8,128)(2,1)}, bf16[512,1024]{1,0:T(8,128)(2,1)}, f32[1,8]{1,0:T(1,128)}, f32[8,4384]{1,0:T(8,128)}, f32[4,18]{1,0:T(4,128...) custom-call(bf16[512,1024]{1,0:T(8,128)(2,1)} %get-tuple-element.28., ...), custom_call_target="tpu_custom_call" | custom-call | tf_op jit(solution)/shard_map/pallas_call | solution.py:1141

commit v3 on v2

--- a/solution.py
+++ b/solution.py
@@ -22,35 +22,74 @@
 THIRD = 384
 MESH = pl.DeviceIdType.MESH
 ORDERS = (("x", "y", "z"), ("y", "z", "x"), ("z", "x", "y"))
-OUT, GATE, EARLY, LATE = 0, 1, 2, 3
+OUT, GATE, EARLY, MID, LATE = 0, 1, 2, 3, 4
+GET_PARTS = {
+    OUT: ((0, 384), (384, 384), (768, 256)),
+    GATE: ((0, 384), (384, 384), (768, 256)),
+    EARLY: ((0, 256), (256, 256), (512, 384)),
+    LATE: ((0, 128), (128, 128), (256, 128)),
+}
+GET_BASE = {GATE: 0, EARLY: 2048, LATE: 3840}
+GET_WIDTH = {OUT: 1024, GATE: 1024, EARLY: 896, LATE: 384}
+SPLIT = 14
+TILES = (
+    (3840, 512),
+    (4352, 256),
+    (2048, 512),
+    (2560, 512),
+    (3072, 512),
+    (3584, 256),
+    (0, 512),
+    (512, 512),
+    (1024, 512),
+    (1536, 512),
+)
 PARTS = {
     OUT: ((0, 512), (512, 256), (768, 256)),
-    GATE: ((0, 256), (256, 256), (512, 512)),
-    EARLY: ((0, 256), (256, 256), (512, 256)),
-    LATE: ((0, 128), (128, 256), (384, 128)),
+    GATE: ((0, 256), (512, 512), (256, 256)),
+    EARLY: ((0, 128), (128, 128), (256, 256)),
+    MID: ((0, 128), (128, 128), (256, 128)),
+    LATE: ((0, 128), (128, 128), (256, 128)),
 }
-GROUPS = {OUT: ((0,), (1, 2)), GATE: ((0, 1), (2,)), EARLY: ((0, 1), (2,)), LATE: ((0, 1, 2),)}
-LOCAL = {OUT: 0, GATE: 1024, EARLY: 2048, LATE: 2816}
-BASE = {GATE: 0, EARLY: 2048, LATE: 3584}
-WIDTH = {GATE: 1024, EARLY: 768, LATE: 512}
-SPLIT = 12
+GROUPS = {
+    OUT: (((0,), 0), ((1, 2), 1)),
+    GATE: (((0, 2), 0), ((1,), 1)),
+    EARLY: (((0, 1, 2), 0),),
+    MID: (((0, 1, 2), 1),),
+    LATE: (((0, 1, 2), 0),),
+}
+LOCAL = {OUT: 0, GATE: 1024, EARLY: 2048, MID: 2560, LATE: 2944}
+BASE = {GATE: 0, EARLY: 2048, MID: 3072, LATE: 3840}
+WIDTH = {OUT: 1024, GATE: 1024, EARLY: 512, MID: 384, LATE: 384}
+BACK_TILES = (
+    (0, 512),
+    (512, 512),
+    (1024, 512),
+    (1536, 512),
+    (2048, 512),
+    (2560, 512),
+    (3072, 512),
+    (3584, 256),
+    (3840, 512),
+    (4352, 256),
+)
+
 eps = 1e-05
 LOG2E = 1.4426950408889634
 highest = lax.Precision.HIGHEST
 
-TILES = (3584, 4096, 2048, 2560, 3072, 0, 512, 1024, 1536)
-BACK_TILES = (0, 512, 1024, 1536, 2048, 2560, 3072, 3584, 4096)
 PLAN = (
     (1, (("dn", 0),)),
     (2, (("own", GATE),)),
     (4, (("dn", 1),)),
-    (6, (("one", OUT), ("dn", 2))),
+    (6, (("dn", 2),)),
+    (7, (("one", OUT),)),
     (8, (("dn", 3),)),
-    (10, (("one", GATE),)),
-    (12, (("two", OUT),)),
-    (13, (("give", EARLY),)),
-    (14, (("dn", 4),)),
-    (15, (("own", EARLY), ("two", GATE))),
+    (9, (("give", EARLY),)),
+    (11, (("one", GATE), ("own", EARLY))),
+    (13, (("two", OUT), ("dn", 4))),
+    (14, (("dn", 5),)),
+    (15, (("two", GATE), ("give", MID), ("dn", 6))),
 )
 
 
@@ -263,53 +302,53 @@
     swap.start()
 
     def held(batch, part, reach):
-        start, width = PARTS[batch][part]
+        start, width = GET_PARTS[batch][part]
         if batch == OUT:
             return full_out.at[chips(at, reach) + (core, slice(None), pl.ds(start, width))]
-        spot = pl.multiple_of(core * WIDTH[batch] + start + BASE[batch], 128)
+        spot = pl.multiple_of(core * GET_WIDTH[batch] + start + GET_BASE[batch], 128)
         return full_in.at[chips(at, reach) + (slice(None), pl.ds(spot, width))]
 
-    flying = {}
+    def wait_bytes(blocks, width, sem):
+        size = 512 if width % 512 == 0 else 128
+        count = blocks * width // size
+        if count > 2 * CHIPS:
+            size, count = 512, blocks * width // 512
+        shape = work.at[pl.ds(0, count), :, pl.ds(0, size)]
+        pltpu.make_async_copy(shape, shape, sem).wait()
+
     drained = []
 
-    def hop(batch, part, phase):
-        target = held(batch, part, ORDERS[part][:phase])
-        source = target
-        if phase == 0 and batch != OUT:
-            start, width = PARTS[batch][part]
-            source = blk.at[:, pl.ds(BASE[batch] // 2 + start, width)]
-        flying[batch, part] = []
-        for step in (1, 2, 3):
-            slot = ((batch * 3 + part) * 3 + phase) * 3 + step - 1
-            copy = remote(source, target, ag_send.at[slot], ag_recv.at[slot], moved(at, ORDERS[part][phase], step))
-            copy.start()
-            flying[batch, part].append(copy)
-            drained.append(copy)
-
-    def landed(batch, part):
-        for copy in flying[batch, part]:
-            copy.wait_recv()
-
-    given = {}
+    def hop(batch, phase):
+        slot = batch * 3 + phase
+        for part in range(3):
+            target = held(batch, part, ORDERS[part][:phase])
+            source = target
+            if phase == 0 and batch != OUT:
+                start, width = GET_PARTS[batch][part]
+                source = blk.at[:, pl.ds(GET_BASE[batch] // 2 + start, width)]
+            for step in (1, 2, 3):
+                peer = moved(at, ORDERS[part][phase], step)
+                remote(source, target, ag_send.at[slot], ag_recv.at[slot], peer).start()
+        drained.append((3 * 4**phase, GET_WIDTH[batch], ag_send.at[slot]))
+
+    def landed(batch, phase):
+        wait_bytes(3 * 4**phase, GET_WIDTH[batch], ag_recv.at[batch * 3 + phase])
 
     def give(batch):
+        landed(batch, 2)
         for part in range(3):
-            landed(batch, part)
             region = held(batch, part, "xyz")
-            slot = batch * 3 + part
-            given[batch, part] = remote(region, region, ag_pass.at[slot], ag_got.at[slot], sibling)
-            given[batch, part].start()
-            drained.append(given[batch, part])
+            remote(region, region, ag_pass.at[batch], ag_got.at[batch], sibling).start()
+        drained.append((CHIPS, GET_WIDTH[batch], ag_pass.at[batch]))
 
     def taken(batch):
-        for part in range(3):
-            given[batch, part].wait_recv()
+        wait_bytes(CHIPS, GET_WIDTH[batch], ag_got.at[batch])
 
     swap.wait()
     stores = []
 
     def begin(batch):
-        base, width = BASE[batch], WIDTH[batch]
+        base, width = GET_BASE[batch], GET_WIDTH[batch]
         lanes = pl.ds(pl.multiple_of(base + core * width, 128), width)
         mine, theirs = wi[:, lanes], other[:, lanes]
         blk[:, base // 2 : base // 2 + width] = jnp.concatenate(
@@ -323,10 +362,9 @@
         stores.append(copy)
 
     def launch(batch, phase):
-        for part in range(3):
-            if phase:
-                landed(batch, part)
-            hop(batch, part, phase)
+        if phase:
+            landed(batch, phase - 1)
+        hop(batch, phase)
 
     begin(LATE)
     begin(EARLY)
@@ -346,28 +384,27 @@
             return work.reshape(4, 4, 2, 4, 16, 512).at[pl.ds(2 * slot, 2)]
         return inner_t.reshape(2, 4, 2, 4, 2, 16, 512).at[:, :, :, :, slot - 2]
 
-    def fetched(slot, start):
-        source = full_in.at[:, :, :, :, :, pl.ds(start, 512)]
-        return pltpu.make_async_copy(source, slot_of(slot), local_sem.at[3 + slot])
+    def fetched(slot, start, width):
+        source = full_in.at[:, :, :, :, :, pl.ds(start, width)]
+        return pltpu.make_async_copy(source, slot_of(slot).at[:, :, :, :, :, pl.ds(0, width)], local_sem.at[3 + slot])
 
     def fetch(i):
-        fetched(i % 4, TILES[i]).start()
+        fetched(i % 4, *TILES[i]).start()
 
     def weight(i):
-        slot = i % 4
-        fetched(slot, TILES[i]).wait()
+        slot, width = i % 4, TILES[i][1]
+        fetched(slot, *TILES[i]).wait()
         if slot < 2:
-            return work[pl.ds(CHIPS * slot, CHIPS)].reshape(D, 512)
-        return inner_t[:, slot - 2].reshape(D, 512)
+            return work[pl.ds(CHIPS * slot, CHIPS), :, :width].reshape(D, width)
+        return inner_t[:, slot - 2, :, :width].reshape(D, width)
 
     give(LATE)
     launch(GATE, 2)
     taken(LATE)
     fetch(1)
     fetch(0)
-    give(EARLY)
     late = weight(1)
-    packed = late[:, 384:]
+    packed = late[:, 128:]
 
     def spread(r, base, count, each):
         pick = (
@@ -388,8 +425,8 @@
         normed_t[j * 8 : j * 8 + 8] = value.T.reshape(8, 16, TOK)
 
     def project(i, weights):
-        width = weights.shape[1]
-        proj[:, TILES[i] : TILES[i] + width] = dot(normed[...], weights)
+        start, width = TILES[i][0], weights.shape[1]
+        proj[:, start : start + width] = dot(normed[...], weights)
 
     def convolve(begin, end):
         @pl.loop(begin, end)
@@ -403,18 +440,18 @@
             act[:, cols] = (pre * sig).astype(low)
             dsilu[:, cols] = (sig * (1.0 + pre * (1.0 - sig))).astype(low)
 
-    project(1, late[:, :384])
+    project(1, late[:, :128])
     project(0, weight(0))
+    give(EARLY)
     taps[...] = jnp.zeros_like(taps)
     for base in (0, XBC // 2):
         for k in range(CONV + 1):
             taps[k : k + 1, base : base + XBC // 2] = spread((3, 4, 5, 6, 2)[k], base, XBC // 2, 18)
     gain[...] = spread(1, 0, INNER, 16)
+    launch(OUT, 2)
     taken(EARLY)
-    for i in (2, 3, 4):
+    for i in (2, 3, 4, 5):
         fetch(i)
-    launch(OUT, 2)
-    give(GATE)
     convolve(SPLIT, XBC // 128)
 
     raw = proj[:, INNER + XBC : INNER + XBC + 128] + heads[0:1, :]
@@ -451,13 +488,16 @@
     mix[...] = mixed
     mix_t[...] = mixed.T
 
-    for i in (2, 3, 4):
+    for i in (2, 3):
         project(i, weight(i))
+    give(GATE)
+    for i in (4, 5):
+        project(i, weight(i))
+    convolve(0, SPLIT)
     taken(GATE)
-    for i in (5, 6, 7, 8):
+    for i in (6, 7, 8, 9):
         fetch(i)
-    convolve(0, SPLIT)
-    for i in (5, 6, 7, 8):
+    for i in (6, 7, 8, 9):
         project(i, weight(i))
     give(OUT)
     q_ref[...] = jnp.zeros_like(q_ref)
@@ -538,9 +578,10 @@
                 rs_pass_copy(*gone.pop()).wait_send()
 
     def rs_give(batch):
-        for slot, group in enumerate(GROUPS[batch]):
+        for group, slot in GROUPS[batch]:
             while users[slot]:
                 rs_pass_copy(*users[slot].pop()).wait_send()
+            origin = PARTS[batch][group[0]][0]
             for half in (0, 1):
                 for part, offset, width, value in grads(batch, group, 1 - core, half):
                     value = value[:, offset : offset + width].astype(low)
@@ -549,7 +590,7 @@
                             16 * m : 16 * m + 16
                         ]
             for part in group:
-                offset = PARTS[batch][part][0] - PARTS[batch][group[0]][0]
+                offset = PARTS[batch][part][0] - origin
                 users[slot].append((batch, part, slot, offset))
                 rs_pass_copy(batch, part, slot, offset).start()
 
@@ -560,7 +601,7 @@
             work.at[pl.ds(CHIPS * slot, CHIPS), :, pl.ds(offset, width)],
             part0.at[:, :, lanes_of(batch, part)],
             rs_pass.at[sem],
-            rs_got.at[sem],
+            rs_got.at[batch],
             sibling,
         )
 
@@ -581,7 +622,7 @@
                 source, target = part1.at[pl.ds(there * 4, 4), :, lanes], recv2.at[pl.ds(4 * step - 4, 4), :, lanes]
             else:
                 source, target = part2.at[pl.ds(there, 1), :, lanes], recv3.at[slot, :, lanes]
-            sem = ((batch * 3 + part) * 3 + stage - 1) * 3 + step - 1
+            sem = batch * 3 + stage - 1
             copies.append(remote(source, target, rs_send.at[sem], rs_recv.at[sem], peer))
         return copies
 
@@ -589,14 +630,16 @@
         for copy in rs_copies(batch, part, stage):
             copy.start()
 
-    def rs_landed(batch, part, stage):
-        for copy in rs_copies(batch, part, stage):
-            copy.wait_recv()
+    def rs_wait(batch, stage, sems):
+        lanes = pl.ds(LOCAL[batch], WIDTH[batch])
+        every = (recv1, recv2, recv3)[stage - 1].at[:, :, lanes]
+        pltpu.make_async_copy(every, every, sems.at[batch * 3 + stage - 1]).wait()
 
     def rs_own(batch):
-        for group in GROUPS[batch]:
-            for part in group:
-                rs_pass_copy(batch, part).wait_recv()
+        lanes = pl.ds(LOCAL[batch], WIDTH[batch])
+        every = part0.at[:, :, lanes]
+        pltpu.make_async_copy(every, every, rs_got.at[batch]).wait()
+        for group, _ in GROUPS[batch]:
             for half in (0, 1):
                 for part, offset, width, value in grads(batch, group, core, half):
                     lanes = lanes_of(batch, part)
@@ -607,9 +650,8 @@
             for part in group:
                 rs_hop(batch, part, 1)
 
-    def rs_one(batch, part):
+    def part_one(batch, part):
         lanes = lanes_of(batch, part)
-        rs_landed(batch, part, 1)
         mine = at[ORDERS[part][2]] * 16
         for i in range(16):
             now = pl.ds(i, 1)
@@ -619,9 +661,8 @@
             part1[now, :, lanes] = value.astype(low)
         rs_hop(batch, part, 2)
 
-    def rs_two(batch, part):
+    def part_two(batch, part):
         lanes = lanes_of(batch, part)
-        rs_landed(batch, part, 2)
         mine = at[ORDERS[part][1]] * 4
         for i in range(4):
             now = pl.ds(i, 1)
@@ -631,9 +672,8 @@
             part2[now, :, lanes] = value.astype(low)
         rs_hop(batch, part, 3)
 
-    def rs_three(batch, part):
+    def part_three(batch, part):
         lanes = lanes_of(batch, part)
-        rs_landed(batch, part, 3)
         value = part2[pl.ds(at[ORDERS[part][0]], 1), :, lanes].astype(full)
         for k in range(3):
             value = value + recv3[pl.ds(k, 1), :, lanes].astype(full)
@@ -650,7 +690,7 @@
     rs_give(OUT)
     taken(OUT)
     while drained:
-        drained.pop().wait_send()
+        wait_bytes(*drained.pop())
     wout = full_out.reshape(INNER, D)
     wide_live = jnp.concatenate([live[...], live[...]], axis=1)
 
@@ -696,12 +736,12 @@
     dnormed = proj.at[:, pl.ds(0, D)]
 
     def back_load(i):
-        fetched(2 + i % 2, BACK_TILES[i]).start()
+        fetched(2 + i % 2, *BACK_TILES[i]).start()
 
     def back_tile(i):
-        start = BACK_TILES[i]
-        fetched(2 + i % 2, start).wait()
-        value = dot_nt(dproj[:, start : start + 512], inner_t[:, i % 2].reshape(D, 512))
+        start, width = BACK_TILES[i]
+        fetched(2 + i % 2, start, width).wait()
+        value = dot_nt(dproj[:, start : start + width], inner_t[:, i % 2, :, :width].reshape(D, width))
         dnormed[...] = value if i == 0 else dnormed[...] + value
         if i + 2 < len(BACK_TILES):
             back_load(i + 2)
@@ -722,6 +762,21 @@
             dx = dx + taps[3 - step : 4 - step, cols] * moved_up
         dproj[:, tile(j, INNER)] = dx.astype(low)
 
+    def rs_one(batch):
+        rs_wait(batch, 1, rs_recv)
+        for part in range(3):
+            part_one(batch, part)
+
+    def rs_two(batch):
+        rs_wait(batch, 2, rs_recv)
+        for part in range(3):
+            part_two(batch, part)
+
+    def rs_three(batch):
+        rs_wait(batch, 3, rs_recv)
+        for part in range(3):
+            part_three(batch, part)
+
     back_ref[...] = jnp.zeros_like(back_ref)
 
     def settle(j):
@@ -746,11 +801,8 @@
                 for action, what in events:
                     if action == "dn":
                         back_tile(what)
-                    elif action in ("give", "own"):
-                        {"give": rs_give, "own": rs_own}[action](what)
                     else:
-                        for part in range(3):
-                            {"one": rs_one, "two": rs_two, "three": rs_three}[action](what, part)
+                        {"give": rs_give, "own": rs_own, "one": rs_one, "two": rs_two}[action](what)
 
         settle(jnp.maximum(j - 1, 0))
         cols = tile(j)
@@ -785,6 +837,7 @@
             back_ref[block * 128 : block * 128 + 128] = value
 
     settle(HEADS // 2 - 1)
+    rs_own(MID)
     masked = jnp.where(row <= column, mix[...], 0.0)
     conv_back(dot(masked.astype(low), act[:, INNER + STATE :]), INNER // 128)
     conv_back(dot(masked.T.astype(low), act[:, INNER : INNER + STATE]), INNER // 128 + 1)
@@ -813,54 +866,55 @@
             axis = ORDERS[part][stage - 1]
             for step in (1, 2, 3):
                 slot = (stage - 1) * 3 + step - 1
-                sem = slot * 3 + part + 1
                 made.append(
                     remote(
                         small_half.at[stage - 1, :, lanes],
                         small_got.at[slot, :, lanes],
-                        small_send.at[sem],
-                        small_recv.at[sem],
+                        small_send.at[stage],
+                        small_recv.at[stage],
                         moved(at, axis, step),
                     )
                 )
         return made
 
     def small_back():
-        return remote(small_half.at[3], small_last, small_send.at[28], small_recv.at[28], sibling)
+        return remote(small_half.at[3], small_last, small_send.at[4], small_recv.at[4], sibling)
+
+    def small_wait(stage, sems):
+        if stage in (0, 4):
+            sems_of = small_other if stage == 0 else small_last
+            pltpu.make_async_copy(sems_of, sems_of, sems.at[stage]).wait()
+        else:
+            every = small_got.at[pl.ds((stage - 1) * 3, 3)]
+            pltpu.make_async_copy(every, every, sems.at[stage]).wait()
 
     def small_add(stage):
+        small_wait(stage, small_recv)
         if stage == 0:
-            small_swap().wait_recv()
             mine = pl.ds(pl.multiple_of(core * HALF, 128), HALF)
             small_half[0] = small_now[:, mine] + small_other[...]
         else:
-            for copy in small_copies(stage):
-                copy.wait_recv()
             value = small_half[stage - 1]
             for k in range(3):
                 value = value + small_got[(stage - 1) * 3 + k]
             small_half[stage] = value
         for copy in small_copies(stage + 1) if stage < 3 else [small_back()]:
             copy.start()
-            drained.append(copy)
-
-    def norm_copies(stage):
-        made = []
+
+    def norm_start(stage):
         for step in (1,) if stage == 0 else (1, 2, 3):
             slot = 0 if stage == 0 else stage * 3 - 3 + step
             peer = moved(at, "cxyz"[stage], step)
-            made.append(remote(norm_now.at[stage], norm_got.at[slot], norm_send.at[slot], norm_recv.at[slot], peer))
-        return made
-
-    def norm_start(stage):
-        for copy in norm_copies(stage):
-            copy.start()
-            drained.append(copy)
+            remote(norm_now.at[stage], norm_got.at[slot], norm_send.at[stage], norm_recv.at[stage], peer).start()
+
+    def norm_wait(stage, sems):
+        every = norm_got.at[pl.ds(0, 1)] if stage == 0 else norm_got.at[pl.ds(stage * 3 - 2, 3)]
+        pltpu.make_async_copy(every, every, sems.at[stage]).wait()
 
     def norm_add(stage):
+        norm_wait(stage, norm_recv)
         value = norm_now[stage]
-        for k, copy in enumerate(norm_copies(stage)):
-            copy.wait_recv()
+        for k in range(1 if stage == 0 else 3):
             value = value + norm_got[0 if stage == 0 else stage * 3 - 2 + k]
         if stage == 3:
             norm_out[...] = value
@@ -868,20 +922,14 @@
             norm_now[stage + 1] = value
             norm_start(stage + 1)
 
-    def drain():
-        while drained:
-            drained.pop().wait_send()
-
     small_swap().start()
-    drained.append(small_swap())
     rs_give(LATE)
-    back_tile(5)
+    back_tile(7)
     small_add(0)
-    back_tile(6)
+    back_tile(8)
     rs_own(LATE)
-    back_tile(7)
+    back_tile(9)
     small_add(1)
-    back_tile(8)
     m_ref[...] = jnp.zeros_like(m_ref)
     for j in range(D // 128):
         cols = slice(j * 128, j * 128 + 128)
@@ -891,8 +939,8 @@
         m_ref[...] += du * norm_gain[:, cols]
     mean = row_sum(m_ref[...]) / D
     norm_start(0)
-    for part in range(3):
-        rs_one(EARLY, part)
+    rs_one(EARLY)
+    rs_one(MID)
     for j in range(D // 128):
         cols = slice(j * 128, j * 128 + 128)
         u = tokens[:, cols].astype(full) * token_scale
@@ -901,28 +949,22 @@
     final = pltpu.make_async_copy(normed, input_grad, local_sem.at[0])
     final.start()
     norm_add(0)
-    for part in range(3):
-        rs_three(OUT, part)
-    for part in range(3):
-        rs_three(GATE, part)
+    rs_three(OUT)
+    rs_three(GATE)
     for batch in (OUT, GATE):
-        for part in range(3):
-            for stage in (1, 2, 3):
-                for copy in rs_copies(batch, part, stage):
-                    copy.wait_send()
+        for stage in (1, 2, 3):
+            rs_wait(batch, stage, rs_send)
     small_add(2)
     norm_add(1)
-    for part in range(3):
-        rs_one(LATE, part)
-    for part in range(3):
-        rs_two(EARLY, part)
+    rs_one(LATE)
+    rs_two(EARLY)
+    rs_two(MID)
     small_add(3)
     norm_add(2)
-    for part in range(3):
-        rs_two(LATE, part)
-    for part in range(3):
-        rs_three(EARLY, part)
-    small_back().wait_recv()
+    rs_two(LATE)
+    rs_three(EARLY)
+    rs_three(MID)
+    small_wait(4, small_recv)
     mine = pl.ds(pl.multiple_of(core * HALF, 128), HALF)
     small_out[:, mine] = small_half[3]
     small_out[:, pl.ds(pl.multiple_of((1 - core) * HALF, 128), HALF)] = small_last[...]
@@ -934,19 +976,19 @@
     norm_add(3)
     outputs.append(pltpu.make_async_copy(norm_out, norm_hbm, edge_sem.at[8]))
     outputs[3].start()
-    drain()
-    for part in range(3):
-        rs_three(LATE, part)
+    for stage in range(5):
+        small_wait(stage, small_send)
+    for stage in range(4):
+        norm_wait(stage, norm_send)
+    rs_three(LATE)
     last = remote(swap_from, swap_to, swap_sem.at[2], swap_sem.at[3], sibling)
     last.start()
-    for batch in (EARLY, LATE):
-        for part in range(3):
-            for stage in (1, 2, 3):
-                for copy in rs_copies(batch, part, stage):
-                    copy.wait_send()
+    for batch in (EARLY, MID, LATE):
+        for stage in (1, 2, 3):
+            rs_wait(batch, stage, rs_send)
     final.wait()
     last.wait()
-    for batch in (GATE, EARLY, LATE):
+    for batch in (GATE, EARLY, MID, LATE):
         base, width = BASE[batch], WIDTH[batch]
         lanes = pl.ds(pl.multiple_of(base + (1 - core) * width, 128), width)
         gi_out[:, lanes] = swap_to[:, base // 2 : base // 2 + width]
@@ -1033,18 +1075,18 @@
             sems((4,)),
             sems((7,)),
             sems((10,)),
-            sems((108,)),
-            sems((108,)),
-            sems((12,)),
-            sems((12,)),
-            sems((108,)),
-            sems((108,)),
-            sems((12,)),
-            sems((12,)),
-            sems((29,)),
-            sems((29,)),
-            sems((10,)),
-            sems((10,)),
+            sems((15,)),
+            sems((15,)),
+            sems((5,)),
+            sems((5,)),
+            sems((15,)),
+            sems((15,)),
+            sems((15,)),
+            sems((5,)),
+            sems((5,)),
+            sems((5,)),
+            sems((4,)),
+            sems((4,)),
         ],
         compiler_params=pltpu.CompilerParams(collective_id=0, has_side_effects=True, vmem_limit_bytes=63 << 20),
     )(lengths, ids, in_shard, wo, tokens, cotangent, params)

time: 149 us -> 138 us (0.926)
  Pallas kernels: 146 us -> 135 us
    pallas_call x1, Pallas kernels: 142 us -> 132 us  [block(): pl.pallas_call(block_kernel, out_shape=(jax.ShapeDtypeStruct((TOK, D), lo...]
where the time goes in v3:
time: 138 us
  Pallas kernels  135 us (98%)
  between operations  1.5 us (1%)
    pallas_call x1, Pallas kernels, block(): pl.pallas_call(block_kernel, out_shape=(jax.ShapeDtypeStruct((TOK, D), lo...  132 us
    pallas_call x1, Pallas kernels, finish(): pl.pallas_call(finish_kernel, out_shape=[jax.ShapeDtypeStruct(out.shape,...  3.03 us

profile of v3, /device:TPU:1, one launch (start us, length us, event | category | flops | bytes accessed | tf_op | source)
XLA Modules:
  0.0 138.2 jit_solution(5818528242184646357)
XLA Ops:
  1.3 1.4 pad_add_fusion.params_hbm
  2.7 132.3 %shard_map.212 = (bf16[512,1024]{1,0:T(8,128)(2,1)}, bf16[512,1024]{1,0:T(8,128)(2,1)}, f32[8,4608]{1,0:T(8,128)}, f32[16,1024]{1,0:T(8,128)}, f32[8,2304]{1,0:T...) custom-call(s32[128]{0:T(128)} %lengths.1, s32[1]{0:T(128)S(6)} %copy.24.ids, ...), custom_call_target="tpu_custom_call" | custom-call | tf_op jit(solution)/shard_map/pallas_call | solution.py:1005
  135.0 3.0 %shard_map.213 = (bf16[512,1024]{1,0:T(8,128)(2,1)}, bf16[512,1024]{1,0:T(8,128)(2,1)}, f32[1,8]{1,0:T(1,128)}, f32[8,4384]{1,0:T(8,128)}, f32[4,18]{1,0:T(4,128...) custom-call(bf16[512,1024]{1,0:T(8,128)(2,1)} %get-tuple-element.28., ...), custom_call_target="tpu_custom_call" | custom-call | tf_op jit(solution)/shard_map/pallas_call | solution.py:1183

commit v4 on v3

--- a/solution.py
+++ b/solution.py
@@ -80,16 +80,12 @@
 
 PLAN = (
     (1, (("dn", 0),)),
-    (2, (("own", GATE),)),
-    (4, (("dn", 1),)),
-    (6, (("dn", 2),)),
-    (7, (("one", OUT),)),
-    (8, (("dn", 3),)),
-    (9, (("give", EARLY),)),
-    (11, (("one", GATE), ("own", EARLY))),
-    (13, (("two", OUT), ("dn", 4))),
-    (14, (("dn", 5),)),
-    (15, (("two", GATE), ("give", MID), ("dn", 6))),
+    (2, (("own", GATE), ("dn", 1))),
+    (4, (("dn", 2), ("dn", 3), ("one", OUT))),
+    (5, (("give", EARLY),)),
+    (6, (("own", EARLY), ("dn", 4), ("one", GATE))),
+    (7, (("dn", 5), ("two", OUT))),
+    (8, (("give", MID), ("dn", 6))),
 )
 
 
@@ -194,7 +190,6 @@
     wi,
     other,
     blk,
-    live,
     skip,
     full_out,
     work,
@@ -279,27 +274,18 @@
     left = lane < HEAD
     row = lax.broadcasted_iota(jnp.int32, (TOK, TOK), 0)
     column = lax.broadcasted_iota(jnp.int32, (TOK, TOK), 1)
-    for copy in inputs:
+    for copy in inputs[:2]:
         copy.wait()
     wi[:, COLS - 256 :] = jnp.zeros((8, 256), full)
     wi[:, :PROJ] = in_shard[...].astype(full)
     wi[:, COLS - 128 :] = params[0:8, :]
-    full_out[here + (core,)] = wo[...]
-    length = lengths[ids[0]]
-    live[...] = (lax.broadcasted_iota(jnp.int32, (TOK, 128), 0) < length).astype(full)
-    m_ref[...] = jnp.zeros_like(m_ref)
-    for j in range(D // 128):
-        x = tokens[:, j * 128 : j * 128 + 128].astype(full)
-        m_ref[...] += x * x
-    token_scale = lax.rsqrt(row_sum(m_ref[...]) / D + eps)
-    owner = lax.broadcasted_iota(jnp.int32, (128, INNER), 1) >> 6
-    repeats = (lax.broadcasted_iota(jnp.int32, (128, INNER), 0) == owner).astype(full)
-    skip[...] = dot(params[8:16, :], repeats, precision=highest)[2:3]
-    heads = params[8:16, :]
     meet()
 
     swap = remote(wi, other, swap_sem.at[0], swap_sem.at[1], sibling)
     swap.start()
+    for copy in inputs[2:]:
+        copy.wait()
+    full_out[here + (core,)] = wo[...]
 
     def held(batch, part, reach):
         start, width = GET_PARTS[batch][part]
@@ -364,14 +350,28 @@
     def launch(batch, phase):
         if phase:
             landed(batch, phase - 1)
+        if phase == 1 and batch != OUT:
+            stores.pop(0).wait()
         hop(batch, phase)
 
     begin(LATE)
     begin(EARLY)
     begin(GATE)
     launch(OUT, 0)
-    for copy in stores:
-        copy.wait()
+    length = lengths[ids[0]]
+
+    def live(width):
+        return (lax.broadcasted_iota(jnp.int32, (TOK, width), 0) < length).astype(full)
+
+    m_ref[...] = jnp.zeros_like(m_ref)
+    for j in range(D // 128):
+        x = tokens[:, j * 128 : j * 128 + 128].astype(full)
+        m_ref[...] += x * x
+    token_scale = lax.rsqrt(row_sum(m_ref[...]) / D + eps)
+    owner = lax.broadcasted_iota(jnp.int32, (128, INNER), 1) >> 6
+    repeats = (lax.broadcasted_iota(jnp.int32, (128, INNER), 0) == owner).astype(full)
+    skip[...] = dot(params[8:16, :], repeats, precision=highest)[2:3]
+    heads = params[8:16, :]
     launch(LATE, 1)
     launch(EARLY, 1)
     launch(LATE, 2)
@@ -442,16 +442,11 @@
 
     project(1, late[:, :128])
     project(0, weight(0))
-    give(EARLY)
     taps[...] = jnp.zeros_like(taps)
     for base in (0, XBC // 2):
         for k in range(CONV + 1):
             taps[k : k + 1, base : base + XBC // 2] = spread((3, 4, 5, 6, 2)[k], base, XBC // 2, 18)
-    gain[...] = spread(1, 0, INNER, 16)
-    launch(OUT, 2)
-    taken(EARLY)
-    for i in (2, 3, 4, 5):
-        fetch(i)
+    give(EARLY)
     convolve(SPLIT, XBC // 128)
 
     raw = proj[:, INNER + XBC : INNER + XBC + 128] + heads[0:1, :]
@@ -488,15 +483,22 @@
     mix[...] = mixed
     mix_t[...] = mixed.T
 
+    taken(EARLY)
+    for i in (2, 3, 4):
+        fetch(i)
+    gain[...] = spread(1, 0, INNER, 16)
+    fetch(5)
+    launch(OUT, 2)
     for i in (2, 3):
         project(i, weight(i))
     give(GATE)
     for i in (4, 5):
         project(i, weight(i))
-    convolve(0, SPLIT)
+    convolve(0, 10)
     taken(GATE)
     for i in (6, 7, 8, 9):
         fetch(i)
+    convolve(10, SPLIT)
     for i in (6, 7, 8, 9):
         project(i, weight(i))
     give(OUT)
@@ -551,7 +553,7 @@
 
     for j in range(D // 128):
         cols = slice(j * 128, j * 128 + 128)
-        normed[:, cols] = (live[...] * cotangent[:, cols].astype(full)).astype(low)
+        normed[:, cols] = (live(128) * cotangent[:, cols].astype(full)).astype(low)
 
     def grads(batch, group, side, half):
         start = PARTS[batch][group[0]][0]
@@ -692,7 +694,6 @@
     while drained:
         wait_bytes(*drained.pop())
     wout = full_out.reshape(INNER, D)
-    wide_live = jnp.concatenate([live[...], live[...]], axis=1)
 
     m_ref[...] = jnp.zeros_like(m_ref)
 
@@ -700,7 +701,7 @@
     def _(j):
         cols = tile(j, 0, 256)
         branch = dot(dproj[:, :INNER], wout[:, cols])
-        block_out[:, cols] = (tokens[:, cols].astype(full) + wide_live * branch).astype(low)
+        block_out[:, cols] = (tokens[:, cols].astype(full) + live(256) * branch).astype(low)
         shares = normed[:, cols].astype(full) * branch
         m_ref[...] += shares[:, :128] + shares[:, 128:]
 
@@ -792,11 +793,11 @@
             dstep_ref[...] = jnp.where(spot, row_sum(jnp.where(mine, direct, 0.0)), dstep_ref[...])
         conv_back(back + skip[:, cols] * dy, j)
 
-    @pl.loop(0, HEADS // 2)
-    def _(j):
+    @pl.loop(0, HEADS // 4 + 1)
+    def _(run):
         for turn, events in PLAN:
 
-            @pl.when(j == turn)
+            @pl.when(run == turn)
             def _(events=events):
                 for action, what in events:
                     if action == "dn":
@@ -804,37 +805,39 @@
                     else:
                         {"give": rs_give, "own": rs_own, "one": rs_one, "two": rs_two}[action](what)
 
-        settle(jnp.maximum(j - 1, 0))
-        cols = tile(j)
-        keys = spread_heads(key_parts, j)
-        v_low = act[:, cols]
-        dy_low = dinner[:, cols].astype(low)
-        own = (jnp.where(left, v_low, jnp.zeros_like(v_low)), jnp.where(left, jnp.zeros_like(v_low), v_low))
-        found = []
-        for block in range(TOK // 128):
-            start, last = block * 128, block * 128 + 128
-            both = dot_nt(jnp.concatenate([own[0][start:last], own[1][start:last]], axis=0), dy_low[start:])
-            halves = []
-            total = None
-            for e in (0, 1):
-                pieces, shares = [], []
-                for later in range(block, TOK // 128):
-                    span = slice(later * 128, later * 128 + 128)
-                    gap = cum_t[2 * j + e, :, span] - keys[start:last, e * 128 : e * 128 + 128]
-                    if later == block:
-                        gap = jnp.where(anti, gap, -1e30)
-                    decay = jnp.exp2(gap)
-                    pieces.append((mix_t[start:last, span] * decay).astype(low))
-                    inside = slice((later - block) * 128, (later - block + 1) * 128)
-                    shares.append(both[e * 128 : e * 128 + 128, inside] * decay)
-                halves.append(jnp.concatenate(pieces, axis=1))
-                share = jnp.concatenate(shares, axis=1)
-                total = share if total is None else total + share
-            mix[start:last, start:] += total
-            given_back = dot(jnp.concatenate(halves, axis=0), dy_low[start:])
-            found.append(jnp.where(left[:128], given_back[:128], given_back[128:]))
-        for block, value in enumerate(found):
-            back_ref[block * 128 : block * 128 + 128] = value
+        @pl.loop(jnp.maximum(2 * run - 1, 0), jnp.minimum(2 * run + 1, HEADS // 2))
+        def _(j):
+            settle(jnp.maximum(j - 1, 0))
+            cols = tile(j)
+            keys = spread_heads(key_parts, j)
+            v_low = act[:, cols]
+            dy_low = dinner[:, cols].astype(low)
+            own = (jnp.where(left, v_low, jnp.zeros_like(v_low)), jnp.where(left, jnp.zeros_like(v_low), v_low))
+            found = []
+            for block in range(TOK // 128):
+                start, last = block * 128, block * 128 + 128
+                both = dot_nt(jnp.concatenate([own[0][start:last], own[1][start:last]], axis=0), dy_low[start:])
+                halves = []
+                total = None
+                for e in (0, 1):
+                    pieces, shares = [], []
+                    for later in range(block, TOK // 128):
+                        span = slice(later * 128, later * 128 + 128)
+                        gap = cum_t[2 * j + e, :, span] - keys[start:last, e * 128 : e * 128 + 128]
+                        if later == block:
+                            gap = jnp.where(anti, gap, -1e30)
+                        decay = jnp.exp2(gap)
+                        pieces.append((mix_t[start:last, span] * decay).astype(low))
+                        inside = slice((later - block) * 128, (later - block + 1) * 128)
+                        shares.append(both[e * 128 : e * 128 + 128, inside] * decay)
+                    halves.append(jnp.concatenate(pieces, axis=1))
+                    share = jnp.concatenate(shares, axis=1)
+                    total = share if total is None else total + share
+                mix[start:last, start:] += total
+                given_back = dot(jnp.concatenate(halves, axis=0), dy_low[start:])
+                found.append(jnp.where(left[:128], given_back[:128], given_back[128:]))
+            for block, value in enumerate(found):
+                back_ref[block * 128 : block * 128 + 128] = value
 
     settle(HEADS // 2 - 1)
     rs_own(MID)
@@ -927,9 +930,9 @@
     back_tile(7)
     small_add(0)
     back_tile(8)
+    back_tile(9)
     rs_own(LATE)
-    back_tile(9)
-    small_add(1)
+    rs_two(GATE)
     m_ref[...] = jnp.zeros_like(m_ref)
     for j in range(D // 128):
         cols = slice(j * 128, j * 128 + 128)
@@ -939,6 +942,7 @@
         m_ref[...] += du * norm_gain[:, cols]
     mean = row_sum(m_ref[...]) / D
     norm_start(0)
+    small_add(1)
     rs_one(EARLY)
     rs_one(MID)
     for j in range(D // 128):
@@ -950,18 +954,18 @@
     final.start()
     norm_add(0)
     rs_three(OUT)
+    small_add(2)
+    rs_one(LATE)
     rs_three(GATE)
     for batch in (OUT, GATE):
         for stage in (1, 2, 3):
             rs_wait(batch, stage, rs_send)
-    small_add(2)
     norm_add(1)
-    rs_one(LATE)
     rs_two(EARLY)
     rs_two(MID)
     small_add(3)
+    rs_two(LATE)
     norm_add(2)
-    rs_two(LATE)
     rs_three(EARLY)
     rs_three(MID)
     small_wait(4, small_recv)
@@ -973,19 +977,21 @@
     for copy in outputs[1:]:
         copy.start()
     rs_free()
+    for stage in range(5):
+        small_wait(stage, small_send)
+    for batch in (EARLY, MID):
+        for stage in (1, 2, 3):
+            rs_wait(batch, stage, rs_send)
+    rs_three(LATE)
+    last = remote(swap_from, swap_to, swap_sem.at[2], swap_sem.at[3], sibling)
+    last.start()
     norm_add(3)
     outputs.append(pltpu.make_async_copy(norm_out, norm_hbm, edge_sem.at[8]))
     outputs[3].start()
-    for stage in range(5):
-        small_wait(stage, small_send)
     for stage in range(4):
         norm_wait(stage, norm_send)
-    rs_three(LATE)
-    last = remote(swap_from, swap_to, swap_sem.at[2], swap_sem.at[3], sibling)
-    last.start()
-    for batch in (EARLY, MID, LATE):
-        for stage in (1, 2, 3):
-            rs_wait(batch, stage, rs_send)
+    for stage in (1, 2, 3):
+        rs_wait(LATE, stage, rs_send)
     final.wait()
     last.wait()
     for batch in (GATE, EARLY, MID, LATE):
@@ -1029,7 +1035,6 @@
             pltpu.VMEM((8, COLS), full),
             pltpu.VMEM((8, COLS), full),
             pltpu.VMEM((16, XBC), low),
-            pltpu.VMEM((TOK, 128), full),
             pltpu.VMEM((1, INNER), full),
             pltpu.VMEM((2, 4, 2, 4, 2, 16, D), low),
             pltpu.VMEM((2 * CHIPS, 16, 512), low),

time: 138 us -> 134 us (0.971)
  Pallas kernels: 135 us -> 131 us
    pallas_call x1, Pallas kernels: 132 us -> 128 us  [block(): pl.pallas_call(block_kernel, out_shape=(jax.ShapeDtypeStruct((TOK, D), lo...]
where the time goes in v4:
time: 134 us
  Pallas kernels  131 us (98%)
  between operations  1.5 us (1%)
  other arithmetic  1.36 us (1%)
    pallas_call x1, Pallas kernels, block(): pl.pallas_call(block_kernel, out_shape=(jax.ShapeDtypeStruct((TOK, D), lo...  128 us
    pallas_call x1, Pallas kernels, finish(): pl.pallas_call(finish_kernel, out_shape=[jax.ShapeDtypeStruct(out.shape,...  3.03 us

profile of v4, /device:TPU:1, one launch (start us, length us, event | category | flops | bytes accessed | tf_op | source)
XLA Modules:
  0.0 133.9 jit_solution(696996679264742004)
XLA Ops:
  1.3 1.4 %pad_add_fusion.params_hbm = f32[16,128]{1,0:T(8,128)} fusion(f32[1,32]{1,0:T(1,128)} %bitcast.12, f32[1,32]{1,0:T(1,128)} %bitcast.13, f32[1,32]{1,0:T(1,128)} %bitcast.14, bf16[4,18]{1,0:T(4,128)(2,1)} %param.18, bf16[1,18]{1,0:T(2,128)(2,1)} %bitcast.15, bf16[1,16]{1,0:T(2,128)(2,1)} %bitcast.16, bf16[1,8]{1,0:T(2,128)(2,1)} %bitcast.17), kind=kLoop, calls=%fused_computation | loop fusion | flops 20480 | bytes 8804 | tf_op jit(solution)/shard_map/add | solution.py:1231
  2.7 128.1 %shard_map.212 = (bf16[512,1024]{1,0:T(8,128)(2,1)}, bf16[512,1024]{1,0:T(8,128)(2,1)}, f32[8,4608]{1,0:T(8,128)}, f32[16,1024]{1,0:T(8,128)}, f32[8,2304]{1,0:T...) custom-call(s32[128]{0:T(128)} %lengths.1, s32[1]{0:T(128)S(6)} %copy.24.ids, ...), custom_call_target="tpu_custom_call" | custom-call | tf_op jit(solution)/shard_map/pallas_call | solution.py:1011
  130.7 3.0 %shard_map.213 = (bf16[512,1024]{1,0:T(8,128)(2,1)}, bf16[512,1024]{1,0:T(8,128)(2,1)}, f32[1,8]{1,0:T(1,128)}, f32[8,4384]{1,0:T(8,128)}, f32[4,18]{1,0:T(4,128...) custom-call(bf16[512,1024]{1,0:T(8,128)(2,1)} %get-tuple-element.28., ...), custom_call_target="tpu_custom_call" | custom-call | tf_op jit(solution)/shard_map/pallas_call | solution.py:1188

commit v5 on v4

--- a/solution.py
+++ b/solution.py
@@ -508,7 +508,6 @@
 
     causal = lax.broadcasted_iota(jnp.int32, (128, 128), 0) >= lax.broadcasted_iota(jnp.int32, (128, 128), 1)
 
-    anti = lax.broadcasted_iota(jnp.int32, (128, 128), 0) <= lax.broadcasted_iota(jnp.int32, (128, 128), 1)
 
     def spread_heads(parts, j):
         line = lax.broadcasted_iota(jnp.int32, (128, 256), 0)
@@ -782,6 +781,8 @@
 
     def settle(j):
         cols = tile(j)
+        lane = lax.broadcasted_iota(jnp.int32, (TOK, 128), 1)
+        left = lane < HEAD
         values, dy, back = act[:, cols].astype(full), dinner[:, cols], back_ref[...]
         direct = values * back
         crossing = dy.astype(low).astype(full) * (y_ref[:, cols] - skip[:, cols] * values) - direct
@@ -810,6 +811,10 @@
             settle(jnp.maximum(j - 1, 0))
             cols = tile(j)
             keys = spread_heads(key_parts, j)
+            left = lax.broadcasted_iota(jnp.int32, (TOK, 128), 1) < HEAD
+            anti = lax.broadcasted_iota(jnp.int32, (128, 128), 0) <= lax.broadcasted_iota(
+                jnp.int32, (128, 128), 1
+            )
             v_low = act[:, cols]
             dy_low = dinner[:, cols].astype(low)
             own = (jnp.where(left, v_low, jnp.zeros_like(v_low)), jnp.where(left, jnp.zeros_like(v_low), v_low))
@@ -954,17 +959,17 @@
     final.start()
     norm_add(0)
     rs_three(OUT)
+    rs_one(LATE)
     small_add(2)
-    rs_one(LATE)
+    norm_add(1)
     rs_three(GATE)
+    rs_two(EARLY)
+    rs_two(MID)
     for batch in (OUT, GATE):
         for stage in (1, 2, 3):
             rs_wait(batch, stage, rs_send)
-    norm_add(1)
-    rs_two(EARLY)
-    rs_two(MID)
+    rs_two(LATE)
     small_add(3)
-    rs_two(LATE)
     norm_add(2)
     rs_three(EARLY)
     rs_three(MID)
@@ -1131,9 +1136,12 @@
     inner_out,
     sem,
 ):
-    pairs = ((small_in, small), (norm_in, norm), (gi_in, gi), (go_in, go), (out_in, out), (grad_in, grad))
+    pairs = [(small_in, small), (norm_in, norm), (gi_in, gi), (go_in, go)]
+    halves = [pl.ds(0, TOK // 2), pl.ds(TOK // 2, TOK // 2)]
+    for source, target in ((out_in, out), (grad_in, grad)):
+        pairs += [(source.at[half, :], target.at[half, :]) for half in halves]
     copies = [pltpu.make_async_copy(source, target, sem.at[i]) for i, (source, target) in enumerate(pairs)]
-    for copy in copies:
+    for copy in copies[:1] + copies[4:] + copies[1:4]:
         copy.start()
     writes = []
 
@@ -1158,10 +1166,10 @@
     write(dt_out, dt_hbm)
     log_out[...] = small[6:7, 128 : 128 + HEADS]
     write(log_out, log_hbm)
-    copies[4].wait()
-    write(out, out_hbm)
-    copies[5].wait()
-    write(grad, grad_hbm)
+    for i, (source, target) in enumerate(((out, out_hbm), (grad, grad_hbm))):
+        for k, half in enumerate(halves):
+            copies[4 + 2 * i + k].wait()
+            write(source.at[half, :], target.at[half, :])
     copies[2].wait()
     gi_out[...] = gi[:, :PROJ]
     write(gi_out, gi_hbm)
@@ -1200,7 +1208,7 @@
             pltpu.VMEM(out.shape, out.dtype),
         ]
         + [pltpu.VMEM(shape, full) for shape in shapes]
-        + [pltpu.SemaphoreType.DMA((17,))],
+        + [pltpu.SemaphoreType.DMA((21,))],
         compiler_params=pltpu.CompilerParams(vmem_limit_bytes=62 << 20),
     )(out, grad, gi, go, small, norm)
 

time: 134 us -> 133 us (level)
  no operation moved by 1% of the time
where the time goes in v5:
time: 133 us
  Pallas kernels  130 us (98%)
  between operations  1.5 us (1%)
  other arithmetic  1.36 us (1%)
    pallas_call x1, Pallas kernels, block(): pl.pallas_call(block_kernel, out_shape=(jax.ShapeDtypeStruct((TOK, D), lo...  127 us
    pallas_call x1, Pallas kernels, finish(): pl.pallas_call(finish_kernel, out_shape=[jax.ShapeDtypeStruct(out.shape,...  2.95 us

profile of v5, /device:TPU:1, one launch (start us, length us, event | category | flops | bytes accessed | tf_op | source)
XLA Modules:
  0.0 133.2 jit_solution(17170660801691024041)
XLA Ops:
  1.3 1.4 %pad_add_fusion.params_hbm = f32[16,128]{1,0:T(8,128)} fusion(f32[1,32]{1,0:T(1,128)} %bitcast.12, f32[1,32]{1,0:T(1,128)} %bitcast.13, f32[1,32]{1,0:T(1,128)} %bitcast.14, bf16[4,18]{1,0:T(4,128)(2,1)} %param.18, bf16[1,18]{1,0:T(2,128)(2,1)} %bitcast.15, bf16[1,16]{1,0:T(2,128)(2,1)} %bitcast.16, bf16[1,8]{1,0:T(2,128)(2,1)} %bitcast.17), kind=kLoop, calls=%fused_computation | loop fusion | flops 20480 | bytes 8804 | tf_op jit(solution)/shard_map/add | solution.py:1239
  2.7 127.3 %shard_map.212 = (bf16[512,1024]{1,0:T(8,128)(2,1)}, bf16[512,1024]{1,0:T(8,128)(2,1)}, f32[8,4608]{1,0:T(8,128)}, f32[16,1024]{1,0:T(8,128)}, f32[8,2304]{1,0:T...) custom-call(s32[128]{0:T(128)} %lengths.1, s32[1]{0:T(128)S(6)} %copy.24.ids, ...), custom_call_target="tpu_custom_call" | custom-call | tf_op jit(solution)/shard_map/pallas_call | solution.py:1016
  130.0 2.9 %shard_map.213 = (bf16[512,1024]{1,0:T(8,128)(2,1)}, bf16[512,1024]{1,0:T(8,128)(2,1)}, f32[1,8]{1,0:T(1,128)}, f32[8,4384]{1,0:T(8,128)}, f32[4,18]{1,0:T(4,128...) custom-call(bf16[512,1024]{1,0:T(8,128)(2,1)} %get-tuple-element.28., ...), custom_call_target="tpu_custom_call" | custom-call | tf_op jit(solution)/shard_map/pallas_call | solution.py:1196

commit v6 on v5

--- a/solution.py
+++ b/solution.py
@@ -25,20 +25,20 @@
 OUT, GATE, EARLY, MID, LATE = 0, 1, 2, 3, 4
 GET_PARTS = {
     OUT: ((0, 384), (384, 384), (768, 256)),
-    GATE: ((0, 384), (384, 384), (768, 256)),
-    EARLY: ((0, 256), (256, 256), (512, 384)),
+    GATE: ((0, 384), (384, 384), (768, 384)),
+    EARLY: ((0, 256), (256, 256), (512, 256)),
     LATE: ((0, 128), (128, 128), (256, 128)),
 }
-GET_BASE = {GATE: 0, EARLY: 2048, LATE: 3840}
-GET_WIDTH = {OUT: 1024, GATE: 1024, EARLY: 896, LATE: 384}
+GET_BASE = {GATE: 0, EARLY: 2304, LATE: 3840}
+GET_WIDTH = {OUT: 1024, GATE: 1152, EARLY: 768, LATE: 384}
 SPLIT = 14
 TILES = (
     (3840, 512),
     (4352, 256),
-    (2048, 512),
-    (2560, 512),
-    (3072, 512),
-    (3584, 256),
+    (2304, 512),
+    (2816, 512),
+    (3328, 512),
+    (2048, 256),
     (0, 512),
     (512, 512),
     (1024, 512),
@@ -299,7 +299,10 @@
         count = blocks * width // size
         if count > 2 * CHIPS:
             size, count = 512, blocks * width // 512
-        shape = work.at[pl.ds(0, count), :, pl.ds(0, size)]
+        if blocks == CHIPS:
+            shape = full_in.at[:, :, :, :, :, pl.ds(0, width)]
+        else:
+            shape = work.at[pl.ds(0, count), :, pl.ds(0, size)]
         pltpu.make_async_copy(shape, shape, sem).wait()
 
     drained = []
@@ -487,18 +490,19 @@
     for i in (2, 3, 4):
         fetch(i)
     gain[...] = spread(1, 0, INNER, 16)
-    fetch(5)
     launch(OUT, 2)
     for i in (2, 3):
         project(i, weight(i))
     give(GATE)
-    for i in (4, 5):
-        project(i, weight(i))
-    convolve(0, 10)
+    project(4, weight(4))
+    convolve(2, 10)
     taken(GATE)
-    for i in (6, 7, 8, 9):
+    for i in (5, 6, 7, 8):
         fetch(i)
     convolve(10, SPLIT)
+    project(5, weight(5))
+    fetch(9)
+    convolve(0, 2)
     for i in (6, 7, 8, 9):
         project(i, weight(i))
     give(OUT)
@@ -846,6 +850,7 @@
 
     settle(HEADS // 2 - 1)
     rs_own(MID)
+    rs_one(EARLY)
     masked = jnp.where(row <= column, mix[...], 0.0)
     conv_back(dot(masked.astype(low), act[:, INNER + STATE :]), INNER // 128)
     conv_back(dot(masked.T.astype(low), act[:, INNER : INNER + STATE]), INNER // 128 + 1)
@@ -948,7 +953,7 @@
     mean = row_sum(m_ref[...]) / D
     norm_start(0)
     small_add(1)
-    rs_one(EARLY)
+    rs_two(EARLY)
     rs_one(MID)
     for j in range(D // 128):
         cols = slice(j * 128, j * 128 + 128)
@@ -963,7 +968,6 @@
     small_add(2)
     norm_add(1)
     rs_three(GATE)
-    rs_two(EARLY)
     rs_two(MID)
     for batch in (OUT, GATE):
         for stage in (1, 2, 3):
@@ -1166,6 +1170,15 @@
     write(dt_out, dt_hbm)
     log_out[...] = small[6:7, 128 : 128 + HEADS]
     write(log_out, log_hbm)
+    owner = lax.broadcasted_iota(jnp.int32, (INNER, 128), 0) >> 6
+    sums = (owner == lax.broadcasted_iota(jnp.int32, (INNER, 128), 1)).astype(jnp.float32)
+    skip_out[...] = dot(small[:, :INNER], sums, precision=highest)[7:8, :HEADS]
+    write(skip_out, skip_hbm)
+    copies[1].wait()
+    line = lax.broadcasted_iota(jnp.int32, (8, 128), 0)
+    row = jnp.sum(jnp.where(line == me // 16, norm[...], 0.0), axis=0, keepdims=True)
+    gain_out[...] = pltpu.roll(row, lax.rem(128 - 8 * lax.rem(me, 16), 128), axis=1)[:, :8]
+    write(gain_out, gain_hbm)
     for i, (source, target) in enumerate(((out, out_hbm), (grad, grad_hbm))):
         for k, half in enumerate(halves):
             copies[4 + 2 * i + k].wait()
@@ -1175,15 +1188,6 @@
     write(gi_out, gi_hbm)
     copies[3].wait()
     write(go, go_hbm)
-    owner = lax.broadcasted_iota(jnp.int32, (INNER, 128), 0) >> 6
-    sums = (owner == lax.broadcasted_iota(jnp.int32, (INNER, 128), 1)).astype(jnp.float32)
-    skip_out[...] = dot(small[:, :INNER], sums, precision=highest)[7:8, :HEADS]
-    write(skip_out, skip_hbm)
-    copies[1].wait()
-    line = lax.broadcasted_iota(jnp.int32, (8, 128), 0)
-    row = jnp.sum(jnp.where(line == me // 16, norm[...], 0.0), axis=0, keepdims=True)
-    gain_out[...] = pltpu.roll(row, lax.rem(128 - 8 * lax.rem(me, 16), 128), axis=1)[:, :8]
-    write(gain_out, gain_hbm)
     for copy in writes:
         copy.wait()
 

time: 133 us -> 138 us (1.038)
  Pallas kernels: 130 us -> 135 us
    pallas_call x1, Pallas kernels: 127 us -> 132 us  [block(): pl.pallas_call(block_kernel, out_shape=(jax.ShapeDtypeStruct((TOK, D), lo...]
where the time goes in v6:
time: 138 us
  Pallas kernels  135 us (98%)
  between operations  1.5 us (1%)
    pallas_call x1, Pallas kernels, block(): pl.pallas_call(block_kernel, out_shape=(jax.ShapeDtypeStruct((TOK, D), lo...  132 us
    pallas_call x1, Pallas kernels, finish(): pl.pallas_call(finish_kernel, out_shape=[jax.ShapeDtypeStruct(out.shape,...  3.1 us

profile of v6, /device:TPU:1, one launch (start us, length us, event | category | flops | bytes accessed | tf_op | source)
XLA Modules:
  0.0 137.8 jit_solution(696896857478073411)
XLA Ops:
  1.3 1.4 pad_add_fusion.params_hbm
  2.7 131.8 %shard_map.212 = (bf16[512,1024]{1,0:T(8,128)(2,1)}, bf16[512,1024]{1,0:T(8,128)(2,1)}, f32[8,4608]{1,0:T(8,128)}, f32[16,1024]{1,0:T(8,128)}, f32[8,2304]{1,0:T...) custom-call(s32[128]{0:T(128)} %lengths.1, s32[1]{0:T(128)S(6)} %copy.24.ids, ...), custom_call_target="tpu_custom_call" | custom-call | tf_op jit(solution)/shard_map/pallas_call | solution.py:1020
  134.5 3.1 %shard_map.213 = (bf16[512,1024]{1,0:T(8,128)(2,1)}, bf16[512,1024]{1,0:T(8,128)(2,1)}, f32[1,8]{1,0:T(1,128)}, f32[8,4384]{1,0:T(8,128)}, f32[4,18]{1,0:T(4,128...) custom-call(bf16[512,1024]{1,0:T(8,128)(2,1)} %get-tuple-element.28., ...), custom_call_target="tpu_custom_call" | custom-call | tf_op jit(solution)/shard_map/pallas_call | solution.py:1200
